TPU v7x, 32 devices: a whole 2x2x4 slice. The times are simulated.
32 devices in a mesh: groups: 2 (over y), tiles: 4 (over z), rep: 2 (over x), sub: 2 (over core).
Axes of the slice: x: 2, y: 2, z: 4, core: 2. Of those that a mesh axis runs over, the one named last changes fastest.
Arguments:
- amplitudes: float32 [8, 2, 6, 64, 1792], P(('groups', 'tiles'), 'rep'), parts along dimension 0, may hold values from -6 to 6
- integrals: float32 [16, 64, 2, 512], P(('groups', 'tiles'), 'sub', 'rep'), parts along dimension 0, may hold values from -0.21875 to 0.21875
- tile_owner: int32 [8, 2, 6], P(('groups', 'tiles'), 'rep'), parts along dimension 0, may hold values from 0 to 3, as said below
Outputs:
- cycle_term: float32 [16, 64, 1792], P(('groups', 'tiles', 'rep'), 'sub'), parts along dimension 0
There are 2 independent parts, one for each index of `groups`. A program takes and returns all parts, laid end to end along the dimension named above; each array names one. Nothing has to cross between parts.
Inputs may be any that keep to these rules, and one draw needn't show every extreme that they name: `tile_owner`: within each storage block t, r no tiles index owns more than 2 tiles, and in every block one tiles index, the same for all blocks, owns exactly 2.
All inputs are finite; a program needn't handle non-finite values.
Results may differ from a plain program's by a relative error of at most 0.0003.
Values sent between devices are 32-bit elements; how exact they have to be, the bound alone decides.
No kernel may reach another device: no remote copies, remote signals or barrier semaphores. Data moves between devices by JAX's collectives and lax.ppermute only.
A program may use at most 128 MiB of HBM per device.

v0:
```python
import jax
import jax.numpy as jnp
from jax import lax
from jax.sharding import PartitionSpec as P

TILE = 64
CAP = 2


def shards(amplitudes, integrals, tile_owner):
    tile_groups = lax.axis_size("tiles")
    stored = amplitudes.reshape(amplitudes.shape[2], amplitudes.shape[3], amplitudes.shape[4])
    owners = tile_owner.reshape(tile_owner.shape[2])
    stored_count = owners.shape[0]
    earlier = jnp.arange(stored_count)[:, None] > jnp.arange(stored_count)[None, :]
    matching = owners[:, None] == owners[None, :]
    ranking = jnp.sum(matching & earlier, axis=1)
    slot_index = owners * CAP + ranking
    out_tiles = integrals.shape[0]
    tile_rows = integrals.shape[1]
    inner_width = integrals.shape[3]
    columns = stored.shape[2]
    matrix = integrals.reshape(out_tiles * tile_rows, inner_width)
    outgoing = jnp.zeros((tile_groups * CAP, TILE, columns), jnp.float32).at[slot_index].set(stored)
    outgoing = outgoing.reshape(tile_groups, CAP, TILE, columns)
    received = lax.all_to_all(outgoing, "tiles", split_axis=0, concat_axis=0, tiled=True)
    flattened = received.reshape(inner_width, received.shape[3])
    product = jnp.dot(
        matrix, flattened, precision=lax.Precision.HIGHEST, preferred_element_type=jnp.float32
    )
    partial_value = product.reshape(out_tiles, tile_rows, received.shape[3])
    summed = lax.psum_scatter(partial_value, "rep", scatter_dimension=0, tiled=True)
    return summed


def solution(mesh):
    return jax.shard_map(
        shards,
        mesh=mesh,
        in_specs=(
            P(("groups", "tiles"), "rep", None, None, None),
            P(("groups", "tiles"), "sub", "rep", None),
            P(("groups", "tiles"), "rep", None),
        ),
        out_specs=P(("groups", "tiles", "rep"), "sub", None),
        check_vma=False,
    )
```

profile of v0, /device:TPU:0, one launch (start us, length us, event | category | flops | bytes accessed | tf_op | source)
XLA Modules:
  0.0 129.9 jit_solution(8877467667000077361)
XLA Ops:
  6.5 0.0 copy-start
  6.5 1.0 convert_reduce_fusion
  7.5 0.7 fusion.1
  8.2 2.1 %broadcast_in_dim.2 = f32[8,64,1792]{2,1,0:T(8,128)} broadcast(f32[]{:T(128)} %constant.4.clone.1), dimensions={} | broadcast | bytes 3670020 | tf_op jit(solution)/shard_map/broadcast_in_dim | solution.py:24
  10.3 0.0 copy-done
  10.4 5.8 %scatter_fusion = f32[8,64,1792]{2,1,0:T(8,128)} fusion(f32[8,64,1792]{2,1,0:T(8,128)} %broadcast_in_dim.2, s32[6]{0:T(128)S(1)} %fusion.1, f32[6,64,1792]{2,1,0:T(8,128)S(1)} %bitcast.19), kind=kCustom, calls=%fused_computation | custom fusion | bytes 8257560 | tf_op jit(solution)/shard_map/scatter | solution.py:24
  16.2 0.0 copy-start.1
  16.2 6.4 %all-to-all-start = ((f32[4,2,64,1792]{3,2,1,0:T(8,128)}), f32[4,2,64,1792]{3,2,1,0:T(8,128)}, u32[]{:S(2)}, u32[]{:S(2)}) async-start(f32[4,2,64,1792]{3,2,1,0:T(8,128)} %bitcast.18), calls=%async_computation | async-start | bytes 7340032 | tf_op jit(solution)/shard_map/all_to_all | solution.py:26
  22.6 0.0 reduce-scatter.2.cloned.1.call-start
  22.6 0.0 copy-done.1
  22.6 82.2 %all-to-all-done = f32[4,2,64,1792]{3,2,1,0:T(8,128)} async-done(((f32[4,2,64,1792]{3,2,1,0:T(8,128)}), f32[4,2,64,1792]{3,2,1,0:T(8,128)}, u32[]{:S(2)}, u32[]{:S(2)}) %all-to-all-start) | async-done | bytes 3670048 | tf_op jit(solution)/shard_map/all_to_all | solution.py:26
  104.8 5.2 %fusion.2 = f32[1792,64]{0,1:T(8,128)} fusion(f32[512,1792]{1,0:T(8,128)} %bitcast.6, f32[64,512]{1,0:T(8,128)S(1)} %bitcast.21), kind=kOutput, calls=%fused_computation.7 | convolution fusion | flops 704643072 | bytes 4259840 | tf_op jit(solution)/shard_map/dot_general | solution.py:28
  110.0 0.0 reduce-scatter.2.cloned.1.call-update
  110.0 13.1 %reduce-scatter.2.cloned.1.call-done = f32[1,32,1792]{2,1,0:T(8,128)} async-done(((f32[2,32,1792]{2,1,0:T(8,128)}), f32[1,32,1792]{2,1,0:T(8,128)}) %reduce-scatter.2.cloned.1.call-update) | async-done | bytes 229392 | tf_op jit(solution)/shard_map/reduce_scatter | solution.py:32
  (1 shorter events, 0.0 us)
Async XLA Ops:
  6.5 3.8 %copy-start = (f32[1,1,6,64,1792]{4,3,2,1,0:T(8,128)S(1)}, f32[1,1,6,64,1792]{4,3,2,1,0:T(8,128)}, u32[]{:S(2)}) copy-start(f32[1,1,6,64,1792]{4,3,2,1,0:T(8,128)} %param.3) | copy-start | bytes 8257540
  16.2 6.4 %copy-start.1 = (f32[2,32,1,512]{3,2,1,0:T(1,128)S(1)}, f32[2,32,1,512]{3,2,1,0:T(1,128)}, u32[]{:S(2)}) copy-start(f32[2,32,1,512]{3,2,1,0:T(1,128)} %param.4) | copy-start | bytes 393220
  16.2 88.6 %all-to-all-start = ((f32[4,2,64,1792]{3,2,1,0:T(8,128)}), f32[4,2,64,1792]{3,2,1,0:T(8,128)}, u32[]{:S(2)}, u32[]{:S(2)}) async-start(f32[4,2,64,1792]{3,2,1,0:T(8,128)} %bitcast.18), calls=%async_computation | async-start | bytes 7340032 | tf_op jit(solution)/shard_map/all_to_all | solution.py:26
  22.6 100.5 %reduce-scatter.2.cloned.1.call-start = ((), (), s32[]{:S(2)}) async-start(), calls=%async_computation.2 | async-start | bytes 688128 | tf_op jit(solution)/shard_map/reduce_scatter | solution.py:32
Sparse Core Ops, SparseCore 0:
  110.1 12.9 reduce-scatter.1
where the time goes:
time: 130 us
  waiting for transfers between devices  95.3 us (73%)
  between operations  13.4 us (10%)
  local copies, waits for them, and re-layouts  8.01 us (6%)
  starting transfers between devices  6.41 us (5%)
  matrix products  5.17 us (4%)
  other arithmetic  1.66 us (1%)
    all_to_all x1, waiting for transfers between devices, shards(): lax.all_to_all(outgoing, 'tiles', split_axis=0, concat_axis=0, tiled=True)  82.2 us
    reduce_scatter x1, waiting for transfers between devices, shards(): lax.psum_scatter(partial_value, 'rep', scatter_dimension=0, tiled=True)  13.1 us
    all_to_all x1, starting transfers between devices, shards(): lax.all_to_all(outgoing, 'tiles', split_axis=0, concat_axis=0, tiled=True)  6.41 us
    scatter x1, local copies, waits for them, and re-layouts, shards(): jnp.zeros((tile_groups * CAP, TILE, columns), jnp.float32).at[slot_index]  5.85 us
    dot_general x1, matrix products, shards(): jnp.dot(matrix, flattened, precision=lax.Precision.HIGHEST, preferred_ele...  5.17 us
  transfers between devices with their start and end apart: 2, of which 2 were waited for; matrix products, arithmetic and copies ran while one was open for 0% of the time, Pallas kernels for 0%

commit v1 on v0

v1 whole, which is shorter than its diff:
```python
import functools

import jax
import jax.numpy as jnp
from jax import lax
from jax.experimental import pallas as pl
from jax.experimental.pallas import tpu as pltpu
from jax.sharding import PartitionSpec as P

TILE = 64
CAP = 2
PAIR = TILE * CAP
VMEM_LIMIT = 32 * 1024 * 1024
ANY = pl.BlockSpec(memory_space=pl.ANY)
VMEM = pl.BlockSpec(memory_space=pltpu.VMEM)
SMEM = pl.BlockSpec(memory_space=pltpu.SMEM)


def f32(*shape):
    return jax.ShapeDtypeStruct(shape, jnp.float32)


def call(kernel, outs, ins, scratch=()):
    return functools.partial(
        pl.pallas_call,
        kernel,
        out_shape=outs,
        in_specs=ins,
        out_specs=jax.tree.map(lambda _: VMEM, outs),
        scratch_shapes=list(scratch),
        compiler_params=pltpu.CompilerParams(vmem_limit_bytes=VMEM_LIMIT),
        cost_estimate=pl.CostEstimate(flops=1, bytes_accessed=1, transcendentals=0),
    )()


def split(value):
    high = value.astype(jnp.bfloat16)
    low = (value - high.astype(jnp.float32)).astype(jnp.bfloat16)
    return high, low


def find(owner, target):
    found = []
    for slot in range(CAP):
        seen, index, filled = jnp.int32(0), jnp.int32(0), jnp.int32(0)
        for k in range(owner.shape[0]):
            match = owner[k] == target
            hit = jnp.logical_and(match, seen == slot)
            index = jnp.where(hit, k, index)
            filled = jnp.where(hit, 1, filled)
            seen = seen + match.astype(jnp.int32)
        found.append((index, filled))
    return found


def exchange(value, axis, distance):
    size = lax.axis_size(axis)
    return lax.ppermute(value, axis, [(i, i ^ distance) for i in range(size)])


def pick_kernel(integrals, *rest):
    *pieces, sems = rest
    here = lax.axis_index("tiles")
    copies = []
    for distance, piece in enumerate(pieces):
        start = pl.multiple_of((here ^ distance) * PAIR, PAIR)
        copies.append(pltpu.make_async_copy(integrals.at[:, pl.ds(start, PAIR)], piece, sems.at[distance]))
    for copy in copies:
        copy.start()
    for copy in copies:
        copy.wait()


def split_kernel(stored, high, low):
    value_high, value_low = split(stored[...])
    high[...] = value_high
    low[...] = value_low


def partial_kernel(distance, owner, piece, high, low, send, own):
    rows = own.shape[0]
    target = lax.axis_index("tiles") ^ distance
    rep = lax.axis_index("rep")
    (first, has_first), (second, has_second) = find(owner, target)
    lane = lax.broadcasted_iota(jnp.int32, (rows, PAIR), 1)
    kept = jnp.where(lane < TILE, has_first, has_second) == 1
    right_high = jnp.concatenate([high[first], high[second]], axis=0)
    right_low = jnp.concatenate([low[first], low[second]], axis=0)
    parts = []
    for pair_of in (1 - rep, rep):
        block = piece[pl.ds(pl.multiple_of(pair_of * rows, rows), rows), :]
        parts.append(jnp.where(kept, block, 0.0))
    left_high, left_low = split(jnp.concatenate(parts, axis=0))
    dot = functools.partial(jnp.dot, preferred_element_type=jnp.float32)
    product = dot(left_high, right_high) + (dot(left_high, right_low) + dot(left_low, right_high))
    send[...] = product[:rows]
    own[...] = product[rows:]


def square_shards(amplitudes, integrals, tile_owner):
    groups = lax.axis_size("tiles")
    stored = amplitudes.reshape(amplitudes.shape[2:])
    owner = tile_owner.reshape(tile_owner.shape[2])
    rows = integrals.shape[1]
    matrix = integrals.reshape(-1, integrals.shape[3])
    columns = stored.shape[2]

    picked = call(
        pick_kernel,
        [f32(matrix.shape[0], PAIR)] * groups,
        [ANY],
        [pltpu.SemaphoreType.DMA((groups,))],
    )(matrix)
    pieces = [picked[0]] + [exchange(picked[e], "tiles", e) for e in range(1, groups)]
    half = jax.ShapeDtypeStruct(stored.shape, jnp.bfloat16)
    high, low = pl.pallas_call(
        split_kernel,
        out_shape=[half, half],
        grid=(stored.shape[0],),
        in_specs=[pl.BlockSpec((1,) + stored.shape[1:], lambda k: (k, 0, 0))],
        out_specs=[pl.BlockSpec((1,) + stored.shape[1:], lambda k: (k, 0, 0))] * 2,
        compiler_params=pltpu.CompilerParams(vmem_limit_bytes=VMEM_LIMIT),
        cost_estimate=pl.CostEstimate(flops=1, bytes_accessed=1, transcendentals=0),
    )(stored)

    sums = {}
    for e in (2, 3, 1, 0):
        send, own = call(functools.partial(partial_kernel, e), [f32(rows, columns)] * 2, [SMEM] + [VMEM] * 3)(
            owner, pieces[e], high, low
        )
        sums[e] = own + exchange(send, "rep", 1)
    out = sums[0]
    for e in (2, 3, 1):
        out = out + exchange(sums[e], "tiles", e)
    return out.reshape(1, rows, columns)


def general_shards(amplitudes, integrals, tile_owner):
    tile_groups = lax.axis_size("tiles")
    stored = amplitudes.reshape(amplitudes.shape[2:])
    owners = tile_owner.reshape(tile_owner.shape[2])
    earlier = jnp.arange(owners.shape[0])[:, None] > jnp.arange(owners.shape[0])[None, :]
    matching = owners[:, None] == owners[None, :]
    slot_index = owners * CAP + jnp.sum(matching & earlier, axis=1)
    out_tiles, tile_rows, _, inner_width = integrals.shape
    columns = stored.shape[2]
    matrix = integrals.reshape(out_tiles * tile_rows, inner_width)
    outgoing = jnp.zeros((tile_groups * CAP, TILE, columns), jnp.float32).at[slot_index].set(stored)
    outgoing = outgoing.reshape(tile_groups, CAP, TILE, columns)
    received = lax.all_to_all(outgoing, "tiles", split_axis=0, concat_axis=0, tiled=True)
    product = jnp.dot(
        matrix, received.reshape(inner_width, columns), precision=lax.Precision.HIGHEST, preferred_element_type=jnp.float32
    )
    partial_value = product.reshape(out_tiles, tile_rows, columns)
    return lax.psum_scatter(partial_value, "rep", scatter_dimension=0, tiled=True)


def solution(mesh):
    small = mesh.shape["tiles"] == 4 and mesh.shape["rep"] == 2
    return jax.shard_map(
        square_shards if small else general_shards,
        mesh=mesh,
        in_specs=(
            P(("groups", "tiles"), "rep", None, None, None),
            P(("groups", "tiles"), "sub", "rep", None),
            P(("groups", "tiles"), "rep", None),
        ),
        out_specs=P(("groups", "tiles", "rep"), "sub", None),
        check_vma=False,
    )
```

time: 130 us -> 44.7 us (0.34)
  waiting for transfers between devices: 95.3 us -> 18.8 us
  between operations: 13.4 us -> 0.07 us
  starting transfers between devices: 6.41 us -> 17.7 us
  local copies, waits for them, and re-layouts: 8.01 us -> 2.78 us
  matrix products: 5.17 us -> 0 us
  Pallas kernels: 0 us -> 4.25 us
    all_to_all x1 -> x0, waiting for transfers between devices: 82.2 us -> none  [shards(): lax.all_to_all(outgoing, 'tiles', split_axis=0, concat_axis=0, tiled=True)]
    ppermute x0 -> x10, waiting for transfers between devices: none -> 18.8 us  [exchange(): return lax.ppermute(value, axis, [(i, i ^ distance) for i in range(size)])]
    ppermute x0 -> x10, starting transfers between devices: none -> 17.7 us  [exchange(): return lax.ppermute(value, axis, [(i, i ^ distance) for i in range(size)])]
    reduce_scatter x1 -> x0, waiting for transfers between devices: 13.1 us -> none  [shards(): lax.psum_scatter(partial_value, 'rep', scatter_dimension=0, tiled=True)]
    all_to_all x1 -> x0, starting transfers between devices: 6.41 us -> none  [shards(): lax.all_to_all(outgoing, 'tiles', split_axis=0, concat_axis=0, tiled=True)]
    scatter x1 -> x0, local copies, waits for them, and re-layouts: 5.85 us -> none  [shards(): jnp.zeros((tile_groups * CAP, TILE, columns), jnp.float32).at[slot_index]]
    dot_general x1 -> x0, matrix products: 5.17 us -> none  [shards(): jnp.dot(matrix, flattened, precision=lax.Precision.HIGHEST, preferred_ele...]
    pallas_call x0 -> x6, Pallas kernels: none -> 4.25 us  [the longest x4 3.61 us: square_shards(): call(functools.partial(partial_kernel, e), [f32(rows, columns)] * 2, [SME...]
  transfers between devices with their start and end apart: 2 -> 10, of which waited for: 2 -> 6; matrix products, arithmetic and copies ran while one was open for 0% -> 0% of each run, Pallas kernels for 0% -> 9%
where the time goes in v1:
time: 44.7 us; the launch traced here: 44.5 us
  waiting for transfers between devices  18.8 us (42%)
  starting transfers between devices  17.7 us (40%)
  Pallas kernels  4.25 us (10%)
  local copies, waits for them, and re-layouts  2.78 us (6%)
  other arithmetic  0.86 us (2%)
    ppermute x10, waiting for transfers between devices, exchange(): return lax.ppermute(value, axis, [(i, i ^ distance) for i in range(size)])  18.8 us
    ppermute x10, starting transfers between devices, exchange(): return lax.ppermute(value, axis, [(i, i ^ distance) for i in range(size)])  17.7 us
    pallas_call x4, Pallas kernels, square_shards(): call(functools.partial(partial_kernel, e), [f32(rows, columns)] * 2, [SME...  3.61 us
    unnamed x5, local copies, waits for them, and re-layouts  2.78 us
  transfers between devices with their start and end apart: 10, of which 6 were waited for; matrix products, arithmetic and copies ran while one was open for 0% of the time, Pallas kernels for 9%

profile of v1, /device:TPU:0, one launch (start us, length us, event | category | flops | bytes accessed | tf_op | source)
XLA Modules:
  0.0 44.5 jit_solution(17099787913795482844)
XLA Ops:
  0.0 0.9 %copy.4 = f32[2,32,1,512]{3,1,2,0:T(8,128)S(1)} copy(f32[2,32,1,512]{3,2,1,0:T(1,128)} %param.4) | data formatting | bytes 262144
  0.9 0.1 shard_map.37
  1.0 3.1 %collective-permute-start.7 = (f32[64,128]{1,0:T(8,128)S(1)}, f32[64,128]{1,0:T(8,128)S(1)}, u32[]{:S(2)}, u32[]{:S(2)}) collective-permute-start(f32[64,128]{1,0:T(8,128)S(1)} %get-tuple-element.30), channel_id=1, source_target_pairs={{0,4},{4,0},{8,12},{12,8},{1,5},{5,1},{9,13},{13,9},{2,6},{6,2},{1... | collective-permute-start | bytes 98312 | tf_op jit(solution)/shard_map/ppermute | solution.py:58
  4.1 2.5 %collective-permute-start.4 = (f32[64,128]{1,0:T(8,128)S(1)}, f32[64,128]{1,0:T(8,128)S(1)}, u32[]{:S(2)}, u32[]{:S(2)}) collective-permute-start(f32[64,128]{1,0:T(8,128)S(1)} %get-tuple-element.27), channel_id=1, source_target_pairs={{0,12},{4,8},{8,4},{12,0},{1,13},{5,9},{9,5},{13,1},{2,14},{6,10},... | collective-permute-start | bytes 98312 | tf_op jit(solution)/shard_map/ppermute | solution.py:58
  6.6 0.1 collective-permute-start.1
  6.7 0.0 copy-start
  6.7 1.8 %copy-done = f32[1,1,6,64,1792]{4,3,2,1,0:T(8,128)S(1)} copy-done((f32[1,1,6,64,1792]{4,3,2,1,0:T(8,128)S(1)}, f32[1,1,6,64,1792]{4,3,2,1,0:T(8,128)}, u32[]{:S(2)}) %copy-start) | copy-done | bytes 2752536
  8.5 0.0 copy-start.1
  8.5 0.6 %shard_map.38 = (bf16[6,64,1792]{2,1,0:T(8,128)(2,1)S(1)}, bf16[6,64,1792]{2,1,0:T(8,128)(2,1)S(1)}) custom-call(f32[6,64,1792]{2,1,0:T(8,128)S(1)} %bitcast.5), custom_call_target="tpu_custom_call" | custom-call | flops 1 | bytes 1 | tf_op jit(solution)/shard_map/pallas_call | solution.py:116
  9.0 0.0 collective-permute-done.7.piece
  9.0 0.1 copy-done.1
  9.1 0.9 %shard_map.42 = (f32[32,1792]{1,0:T(8,128)S(1)}, f32[32,1792]{1,0:T(8,128)S(1)}) custom-call(s32[6]{0:T(128)S(1)} %bitcast.7, f32[64,128]{1,0:T(8,128)S(1)} %collective-permute-done.7.piece, bf16[6,64,1792]{2,1,0:T(8,128)(2,1)S(1)} %get-tuple-element.20.high, bf16[6,64,1792]{2,1,0:T(8,128)(2,1)S(1)} %get-tuple-element.21.low), custom_call_target="tpu_custom_call" | custom-call | flops 1 | bytes 1 | tf_op jit(solution)/shard_map/pallas_call | solution.py:128
  10.0 1.6 %collective-permute-start.8 = (f32[32,1792]{1,0:T(8,128)S(1)}, f32[32,1792]{1,0:T(8,128)S(1)}, u32[]{:S(2)}, u32[]{:S(2)}) collective-permute-start(f32[32,1792]{1,0:T(8,128)S(1)} %get-tuple-element.32), channel_id=1, source_target_pairs={{0,2},{2,0},{1,3},{3,1},{4,6},{6,4},{5,7},{7,5},{8,10},{10,8},{9,1... | collective-permute-start | bytes 688136 | tf_op jit(solution)/shard_map/ppermute | solution.py:58
  11.6 0.0 collective-permute-done.4.piece
  11.6 0.9 %shard_map.41 = (f32[32,1792]{1,0:T(8,128)S(1)}, f32[32,1792]{1,0:T(8,128)S(1)}) custom-call(s32[6]{0:T(128)S(1)} %bitcast.8, f32[64,128]{1,0:T(8,128)S(1)} %collective-permute-done.4.piece, bf16[6,64,1792]{2,1,0:T(8,128)(2,1)S(1)} %get-tuple-element.20.high, bf16[6,64,1792]{2,1,0:T(8,128)(2,1)S(1)} %get-tuple-element.21.low), custom_call_target="tpu_custom_call" | custom-call | flops 1 | bytes 1 | tf_op jit(solution)/shard_map/pallas_call | solution.py:128
  12.5 0.6 %collective-permute-start.5 = (f32[32,1792]{1,0:T(8,128)S(1)}, f32[32,1792]{1,0:T(8,128)S(1)}, u32[]{:S(2)}, u32[]{:S(2)}) collective-permute-start(f32[32,1792]{1,0:T(8,128)S(1)} %get-tuple-element.29), channel_id=1, source_target_pairs={{0,2},{2,0},{1,3},{3,1},{4,6},{6,4},{5,7},{7,5},{8,10},{10,8},{9,1... | collective-permute-start | bytes 688136 | tf_op jit(solution)/shard_map/ppermute | solution.py:58
  13.1 0.0 collective-permute-done.1.piece
  13.1 0.9 %shard_map.40 = (f32[32,1792]{1,0:T(8,128)S(1)}, f32[32,1792]{1,0:T(8,128)S(1)}) custom-call(s32[6]{0:T(128)S(1)} %bitcast.9, f32[64,128]{1,0:T(8,128)S(1)} %collective-permute-done.1.piece, bf16[6,64,1792]{2,1,0:T(8,128)(2,1)S(1)} %get-tuple-element.20.high, bf16[6,64,1792]{2,1,0:T(8,128)(2,1)S(1)} %get-tuple-element.21.low), custom_call_target="tpu_custom_call" | custom-call | flops 1 | bytes 1 | tf_op jit(solution)/shard_map/pallas_call | solution.py:128
  14.0 1.6 %collective-permute-start.2 = (f32[32,1792]{1,0:T(8,128)S(1)}, f32[32,1792]{1,0:T(8,128)S(1)}, u32[]{:S(2)}, u32[]{:S(2)}) collective-permute-start(f32[32,1792]{1,0:T(8,128)S(1)} %get-tuple-element.26), channel_id=1, source_target_pairs={{0,2},{2,0},{1,3},{3,1},{4,6},{6,4},{5,7},{7,5},{8,10},{10,8},{9,1... | collective-permute-start | bytes 688136 | tf_op jit(solution)/shard_map/ppermute | solution.py:58
  15.6 0.9 %shard_map.39 = (f32[32,1792]{1,0:T(8,128)S(1)}, f32[32,1792]{1,0:T(8,128)S(1)}) custom-call(s32[6]{0:T(128)S(1)} %bitcast.10, f32[64,128]{1,0:T(8,128)S(1)} %get-tuple-element.19.piece, bf16[6,64,1792]{2,1,0:T(8,128)(2,1)S(1)} %get-tuple-element.20.high, bf16[6,64,1792]{2,1,0:T(8,128)(2,1)S(1)} %get-tuple-element.21.low), custom_call_target="tpu_custom_call" | custom-call | flops 1 | bytes 1 | tf_op jit(solution)/shard_map/pallas_call | solution.py:128
  16.5 0.6 %collective-permute-start = (f32[32,1792]{1,0:T(8,128)S(1)}, f32[32,1792]{1,0:T(8,128)S(1)}, u32[]{:S(2)}, u32[]{:S(2)}) collective-permute-start(f32[32,1792]{1,0:T(8,128)S(1)} %get-tuple-element.23), channel_id=1, source_target_pairs={{0,2},{2,0},{1,3},{3,1},{4,6},{6,4},{5,7},{7,5},{8,10},{10,8},{9,1... | collective-permute-start | bytes 688136 | tf_op jit(solution)/shard_map/ppermute | solution.py:58
  17.1 1.6 %collective-permute-done.8 = f32[32,1792]{1,0:T(8,128)S(1)} collective-permute-done((f32[32,1792]{1,0:T(8,128)S(1)}, f32[32,1792]{1,0:T(8,128)S(1)}, u32[]{:S(2)}, u32[]{:S(2)}) %collective-permute-start.8) | collective-permute-done | bytes 229408 | tf_op jit(solution)/shard_map/ppermute | solution.py:58
  18.7 1.9 %collective-permute-start.9 = (f32[32,1792]{1,0:T(8,128)S(1)}, f32[32,1792]{1,0:T(8,128)S(1)}, u32[]{:S(2)}, u32[]{:S(2)}) collective-permute-start(f32[32,1792]{1,0:T(8,128)S(1)} %add.26), channel_id=1, source_target_pairs={{0,4},{4,0},{8,12},{12,8},{1,5},{5,1},{9,13},{13,9},{2,6},{6,2},{1... | collective-permute-start | bytes 688136 | tf_op jit(solution)/shard_map/ppermute | solution.py:58
  20.5 3.0 %collective-permute-done.5 = f32[32,1792]{1,0:T(8,128)S(1)} collective-permute-done((f32[32,1792]{1,0:T(8,128)S(1)}, f32[32,1792]{1,0:T(8,128)S(1)}, u32[]{:S(2)}, u32[]{:S(2)}) %collective-permute-start.5) | collective-permute-done | bytes 229408 | tf_op jit(solution)/shard_map/ppermute | solution.py:58
  23.6 3.0 %collective-permute-start.6 = (f32[32,1792]{1,0:T(8,128)S(1)}, f32[32,1792]{1,0:T(8,128)S(1)}, u32[]{:S(2)}, u32[]{:S(2)}) collective-permute-start(f32[32,1792]{1,0:T(8,128)S(1)} %add.24), channel_id=1, source_target_pairs={{0,12},{4,8},{8,4},{12,0},{1,13},{5,9},{9,5},{13,1},{2,14},{6,10},... | collective-permute-start | bytes 688136 | tf_op jit(solution)/shard_map/ppermute | solution.py:58
  26.6 1.9 %collective-permute-done.2 = f32[32,1792]{1,0:T(8,128)S(1)} collective-permute-done((f32[32,1792]{1,0:T(8,128)S(1)}, f32[32,1792]{1,0:T(8,128)S(1)}, u32[]{:S(2)}, u32[]{:S(2)}) %collective-permute-start.2) | collective-permute-done | bytes 229408 | tf_op jit(solution)/shard_map/ppermute | solution.py:58
  28.5 2.9 %collective-permute-start.3 = (f32[32,1792]{1,0:T(8,128)S(1)}, f32[32,1792]{1,0:T(8,128)S(1)}, u32[]{:S(2)}, u32[]{:S(2)}) collective-permute-start(f32[32,1792]{1,0:T(8,128)S(1)} %add.22), channel_id=1, source_target_pairs={{0,8},{4,12},{8,0},{12,4},{1,9},{5,13},{9,1},{13,5},{2,10},{6,14},... | collective-permute-start | bytes 688136 | tf_op jit(solution)/shard_map/ppermute | solution.py:58
  31.4 0.2 collective-permute-done
  31.6 0.0 collective-permute-done.9
  31.6 2.7 %collective-permute-done.6 = f32[32,1792]{1,0:T(8,128)S(1)} collective-permute-done((f32[32,1792]{1,0:T(8,128)S(1)}, f32[32,1792]{1,0:T(8,128)S(1)}, u32[]{:S(2)}, u32[]{:S(2)}) %collective-permute-start.6) | collective-permute-done | bytes 229408 | tf_op jit(solution)/shard_map/ppermute | solution.py:58
  34.4 9.4 %collective-permute-done.3 = f32[32,1792]{1,0:T(8,128)S(1)} collective-permute-done((f32[32,1792]{1,0:T(8,128)S(1)}, f32[32,1792]{1,0:T(8,128)S(1)}, u32[]{:S(2)}, u32[]{:S(2)}) %collective-permute-start.3) | collective-permute-done | bytes 229408 | tf_op jit(solution)/shard_map/ppermute | solution.py:58
  43.8 0.8 %add_bitcast_fusion = f32[1,32,1792]{2,1,0:T(8,128)} fusion(f32[32,1792]{1,0:T(8,128)S(1)} %collective-permute-done.9, f32[32,1792]{1,0:T(8,128)S(1)} %collective-permute-done.6, f32[32,1792]{1,0:T(8,128)S(1)} %collective-permute-done.3, f32[32,1792]{1,0:T(8,128)S(1)} %get-tuple-element.22, f32[32,1792]{1,0:T(8,128)S(1)} %collective-permute-done), kind=kLoop, calls=%fused_computation | loop fusion | flops 229376 | bytes 1376256 | tf_op jit(solution)/shard_map/reshape | solution.py:135
  (3 shorter events, 0.1 us)
Async XLA Ops:
  1.0 8.0 %collective-permute-start.7 = (f32[64,128]{1,0:T(8,128)S(1)}, f32[64,128]{1,0:T(8,128)S(1)}, u32[]{:S(2)}, u32[]{:S(2)}) collective-permute-start(f32[64,128]{1,0:T(8,128)S(1)} %get-tuple-element.30), channel_id=1, source_target_pairs={{0,4},{4,0},{8,12},{12,8},{1,5},{5,1},{9,13},{13,9},{2,6},{6,2},{1... | collective-permute-start | bytes 98312 | tf_op jit(solution)/shard_map/ppermute | solution.py:58
  4.1 7.5 %collective-permute-start.4 = (f32[64,128]{1,0:T(8,128)S(1)}, f32[64,128]{1,0:T(8,128)S(1)}, u32[]{:S(2)}, u32[]{:S(2)}) collective-permute-start(f32[64,128]{1,0:T(8,128)S(1)} %get-tuple-element.27), channel_id=1, source_target_pairs={{0,12},{4,8},{8,4},{12,0},{1,13},{5,9},{9,5},{13,1},{2,14},{6,10},... | collective-permute-start | bytes 98312 | tf_op jit(solution)/shard_map/ppermute | solution.py:58
  6.6 6.5 %collective-permute-start.1 = (f32[64,128]{1,0:T(8,128)S(1)}, f32[64,128]{1,0:T(8,128)S(1)}, u32[]{:S(2)}, u32[]{:S(2)}) collective-permute-start(f32[64,128]{1,0:T(8,128)S(1)} %get-tuple-element.24), channel_id=1, source_target_pairs={{0,8},{4,12},{8,0},{12,4},{1,9},{5,13},{9,1},{13,5},{2,10},{6,14},... | collective-permute-start | bytes 98312 | tf_op jit(solution)/shard_map/ppermute | solution.py:58
  6.7 1.8 %copy-start = (f32[1,1,6,64,1792]{4,3,2,1,0:T(8,128)S(1)}, f32[1,1,6,64,1792]{4,3,2,1,0:T(8,128)}, u32[]{:S(2)}) copy-start(f32[1,1,6,64,1792]{4,3,2,1,0:T(8,128)} %param.3) | copy-start | bytes 8257540
  8.5 0.7 %copy-start.1 = (s32[1,1,6]{2,1,0:T(1,128)S(1)}, s32[1,1,6]{2,1,0:T(1,128)}, u32[]{:S(2)}) copy-start(s32[1,1,6]{2,1,0:T(1,128)} %param.5) | copy-start | bytes 76
  10.0 8.6 %collective-permute-start.8 = (f32[32,1792]{1,0:T(8,128)S(1)}, f32[32,1792]{1,0:T(8,128)S(1)}, u32[]{:S(2)}, u32[]{:S(2)}) collective-permute-start(f32[32,1792]{1,0:T(8,128)S(1)} %get-tuple-element.32), channel_id=1, source_target_pairs={{0,2},{2,0},{1,3},{3,1},{4,6},{6,4},{5,7},{7,5},{8,10},{10,8},{9,1... | collective-permute-start | bytes 688136 | tf_op jit(solution)/shard_map/ppermute | solution.py:58
  12.5 11.1 %collective-permute-start.5 = (f32[32,1792]{1,0:T(8,128)S(1)}, f32[32,1792]{1,0:T(8,128)S(1)}, u32[]{:S(2)}, u32[]{:S(2)}) collective-permute-start(f32[32,1792]{1,0:T(8,128)S(1)} %get-tuple-element.29), channel_id=1, source_target_pairs={{0,2},{2,0},{1,3},{3,1},{4,6},{6,4},{5,7},{7,5},{8,10},{10,8},{9,1... | collective-permute-start | bytes 688136 | tf_op jit(solution)/shard_map/ppermute | solution.py:58
  14.0 14.5 %collective-permute-start.2 = (f32[32,1792]{1,0:T(8,128)S(1)}, f32[32,1792]{1,0:T(8,128)S(1)}, u32[]{:S(2)}, u32[]{:S(2)}) collective-permute-start(f32[32,1792]{1,0:T(8,128)S(1)} %get-tuple-element.26), channel_id=1, source_target_pairs={{0,2},{2,0},{1,3},{3,1},{4,6},{6,4},{5,7},{7,5},{8,10},{10,8},{9,1... | collective-permute-start | bytes 688136 | tf_op jit(solution)/shard_map/ppermute | solution.py:58
  16.5 15.1 %collective-permute-start = (f32[32,1792]{1,0:T(8,128)S(1)}, f32[32,1792]{1,0:T(8,128)S(1)}, u32[]{:S(2)}, u32[]{:S(2)}) collective-permute-start(f32[32,1792]{1,0:T(8,128)S(1)} %get-tuple-element.23), channel_id=1, source_target_pairs={{0,2},{2,0},{1,3},{3,1},{4,6},{6,4},{5,7},{7,5},{8,10},{10,8},{9,1... | collective-permute-start | bytes 688136 | tf_op jit(solution)/shard_map/ppermute | solution.py:58
  18.7 13.0 %collective-permute-start.9 = (f32[32,1792]{1,0:T(8,128)S(1)}, f32[32,1792]{1,0:T(8,128)S(1)}, u32[]{:S(2)}, u32[]{:S(2)}) collective-permute-start(f32[32,1792]{1,0:T(8,128)S(1)} %add.26), channel_id=1, source_target_pairs={{0,4},{4,0},{8,12},{12,8},{1,5},{5,1},{9,13},{13,9},{2,6},{6,2},{1... | collective-permute-start | bytes 688136 | tf_op jit(solution)/shard_map/ppermute | solution.py:58
  23.6 10.8 %collective-permute-start.6 = (f32[32,1792]{1,0:T(8,128)S(1)}, f32[32,1792]{1,0:T(8,128)S(1)}, u32[]{:S(2)}, u32[]{:S(2)}) collective-permute-start(f32[32,1792]{1,0:T(8,128)S(1)} %add.24), channel_id=1, source_target_pairs={{0,12},{4,8},{8,4},{12,0},{1,13},{5,9},{9,5},{13,1},{2,14},{6,10},... | collective-permute-start | bytes 688136 | tf_op jit(solution)/shard_map/ppermute | solution.py:58
  28.5 15.2 %collective-permute-start.3 = (f32[32,1792]{1,0:T(8,128)S(1)}, f32[32,1792]{1,0:T(8,128)S(1)}, u32[]{:S(2)}, u32[]{:S(2)}) collective-permute-start(f32[32,1792]{1,0:T(8,128)S(1)} %add.22), channel_id=1, source_target_pairs={{0,8},{4,12},{8,0},{12,4},{1,9},{5,13},{9,1},{13,5},{2,10},{6,14},... | collective-permute-start | bytes 688136 | tf_op jit(solution)/shard_map/ppermute | solution.py:58

commit v2 on v1

--- a/solution.py
+++ b/solution.py
@@ -20,7 +20,7 @@
     return jax.ShapeDtypeStruct(shape, jnp.float32)
 
 
-def call(kernel, outs, ins, scratch=()):
+def call(kernel, outs, ins, scratch=(), flops=1):
     return functools.partial(
         pl.pallas_call,
         kernel,
@@ -29,7 +29,7 @@
         out_specs=jax.tree.map(lambda _: VMEM, outs),
         scratch_shapes=list(scratch),
         compiler_params=pltpu.CompilerParams(vmem_limit_bytes=VMEM_LIMIT),
-        cost_estimate=pl.CostEstimate(flops=1, bytes_accessed=1, transcendentals=0),
+        cost_estimate=pl.CostEstimate(flops=flops, bytes_accessed=1, transcendentals=0),
     )()
 
 
@@ -110,6 +110,7 @@
         [f32(matrix.shape[0], PAIR)] * groups,
         [ANY],
         [pltpu.SemaphoreType.DMA((groups,))],
+        10**10,
     )(matrix)
     pieces = [picked[0]] + [exchange(picked[e], "tiles", e) for e in range(1, groups)]
     half = jax.ShapeDtypeStruct(stored.shape, jnp.bfloat16)
@@ -124,13 +125,13 @@
     )(stored)
 
     sums = {}
-    for e in (2, 3, 1, 0):
+    for e in (1, 3, 2, 0):
         send, own = call(functools.partial(partial_kernel, e), [f32(rows, columns)] * 2, [SMEM] + [VMEM] * 3)(
             owner, pieces[e], high, low
         )
         sums[e] = own + exchange(send, "rep", 1)
     out = sums[0]
-    for e in (2, 3, 1):
+    for e in (1, 3, 2):
         out = out + exchange(sums[e], "tiles", e)
     return out.reshape(1, rows, columns)
 

time: 44.7 us -> 37.8 us (0.85)
  waiting for transfers between devices: 18.8 us -> 11.8 us
  starting transfers between devices: 17.7 us -> 19.8 us
  local copies, waits for them, and re-layouts: 2.78 us -> 0.92 us
    ppermute x10, waiting for transfers between devices: 18.8 us -> 11.8 us  [exchange(): return lax.ppermute(value, axis, [(i, i ^ distance) for i in range(size)])]
    ppermute x10, starting transfers between devices: 17.7 us -> 19.8 us  [exchange(): return lax.ppermute(value, axis, [(i, i ^ distance) for i in range(size)])]
    unnamed x5, local copies, waits for them, and re-layouts: 2.78 us -> 0.92 us
  transfers between devices with their start and end apart: 10 -> 10, of which waited for: 6 -> 7; matrix products, arithmetic and copies ran while one was open for 0% -> 0% of each run, Pallas kernels for 9% -> 11%
where the time goes in v2:
time: 37.8 us; the launch traced here: 37.7 us
  starting transfers between devices  19.8 us (52%)
  waiting for transfers between devices  11.8 us (31%)
  Pallas kernels  4.25 us (11%)
  local copies, waits for them, and re-layouts  0.92 us (2%)
  other arithmetic  0.86 us (2%)
    ppermute x10, starting transfers between devices, exchange(): return lax.ppermute(value, axis, [(i, i ^ distance) for i in range(size)])  19.8 us
    ppermute x10, waiting for transfers between devices, exchange(): return lax.ppermute(value, axis, [(i, i ^ distance) for i in range(size)])  11.8 us
    pallas_call x4, Pallas kernels, square_shards(): call(functools.partial(partial_kernel, e), [f32(rows, columns)] * 2, [SME...  3.61 us
    unnamed x5, local copies, waits for them, and re-layouts  0.92 us
    reshape x1, other arithmetic, square_shards(): return out.reshape(1, rows, columns)  0.76 us
  transfers between devices with their start and end apart: 10, of which 7 were waited for; matrix products, arithmetic and copies ran while one was open for 0% of the time, Pallas kernels for 11%

profile of v2, /device:TPU:0, one launch (start us, length us, event | category | flops | bytes accessed | tf_op | source)
XLA Modules:
  0.0 37.7 jit_solution(7262139129446689209)
XLA Ops:
  0.0 0.9 %copy.4 = f32[2,32,1,512]{3,1,2,0:T(8,128)S(1)} copy(f32[2,32,1,512]{3,2,1,0:T(1,128)} %param.4) | data formatting | bytes 262144
  0.9 0.0 copy-start
  0.9 0.1 shard_map.37
  1.0 4.1 %collective-permute-start.7 = (f32[64,128]{1,0:T(8,128)S(1)}, f32[64,128]{1,0:T(8,128)S(1)}, u32[]{:S(2)}, u32[]{:S(2)}) collective-permute-start(f32[64,128]{1,0:T(8,128)S(1)} %get-tuple-element.30), channel_id=1, source_target_pairs={{0,8},{4,12},{8,0},{12,4},{1,9},{5,13},{9,1},{13,5},{2,10},{6,14},... | collective-permute-start | bytes 98312 | tf_op jit(solution)/shard_map/ppermute | solution.py:58
  5.1 1.3 %collective-permute-start.4 = (f32[64,128]{1,0:T(8,128)S(1)}, f32[64,128]{1,0:T(8,128)S(1)}, u32[]{:S(2)}, u32[]{:S(2)}) collective-permute-start(f32[64,128]{1,0:T(8,128)S(1)} %get-tuple-element.27), channel_id=1, source_target_pairs={{0,12},{4,8},{8,4},{12,0},{1,13},{5,9},{9,5},{13,1},{2,14},{6,10},... | collective-permute-start | bytes 98312 | tf_op jit(solution)/shard_map/ppermute | solution.py:58
  6.5 0.2 collective-permute-start.1
  6.7 0.0 copy-done
  6.7 0.0 copy-start.1
  6.7 0.6 %shard_map.38 = (bf16[6,64,1792]{2,1,0:T(8,128)(2,1)S(1)}, bf16[6,64,1792]{2,1,0:T(8,128)(2,1)S(1)}) custom-call(f32[6,64,1792]{2,1,0:T(8,128)S(1)} %bitcast.5), custom_call_target="tpu_custom_call" | custom-call | flops 1 | bytes 1 | tf_op jit(solution)/shard_map/pallas_call | solution.py:117
  7.3 0.1 collective-permute-done.7.piece
  7.4 0.0 copy-done.1
  7.4 0.9 %shard_map.42 = (f32[32,1792]{1,0:T(8,128)S(1)}, f32[32,1792]{1,0:T(8,128)S(1)}) custom-call(s32[6]{0:T(128)S(1)} %bitcast.7, f32[64,128]{1,0:T(8,128)S(1)} %collective-permute-done.7.piece, bf16[6,64,1792]{2,1,0:T(8,128)(2,1)S(1)} %get-tuple-element.20.high, bf16[6,64,1792]{2,1,0:T(8,128)(2,1)S(1)} %get-tuple-element.21.low), custom_call_target="tpu_custom_call" | custom-call | flops 1 | bytes 1 | tf_op jit(solution)/shard_map/pallas_call | solution.py:129
  8.3 1.8 %collective-permute-start.8 = (f32[32,1792]{1,0:T(8,128)S(1)}, f32[32,1792]{1,0:T(8,128)S(1)}, u32[]{:S(2)}, u32[]{:S(2)}) collective-permute-start(f32[32,1792]{1,0:T(8,128)S(1)} %get-tuple-element.32), channel_id=1, source_target_pairs={{0,2},{2,0},{1,3},{3,1},{4,6},{6,4},{5,7},{7,5},{8,10},{10,8},{9,1... | collective-permute-start | bytes 688136 | tf_op jit(solution)/shard_map/ppermute | solution.py:58
  10.0 0.8 %collective-permute-done.4.piece = f32[64,128]{1,0:T(8,128)S(1)} collective-permute-done((f32[64,128]{1,0:T(8,128)S(1)}, f32[64,128]{1,0:T(8,128)S(1)}, u32[]{:S(2)}, u32[]{:S(2)}) %collective-permute-start.4) | collective-permute-done | bytes 32800 | tf_op jit(solution)/shard_map/ppermute | solution.py:58
  10.8 0.9 %shard_map.41 = (f32[32,1792]{1,0:T(8,128)S(1)}, f32[32,1792]{1,0:T(8,128)S(1)}) custom-call(s32[6]{0:T(128)S(1)} %bitcast.8, f32[64,128]{1,0:T(8,128)S(1)} %collective-permute-done.4.piece, bf16[6,64,1792]{2,1,0:T(8,128)(2,1)S(1)} %get-tuple-element.20.high, bf16[6,64,1792]{2,1,0:T(8,128)(2,1)S(1)} %get-tuple-element.21.low), custom_call_target="tpu_custom_call" | custom-call | flops 1 | bytes 1 | tf_op jit(solution)/shard_map/pallas_call | solution.py:129
  11.7 1.6 %collective-permute-start.5 = (f32[32,1792]{1,0:T(8,128)S(1)}, f32[32,1792]{1,0:T(8,128)S(1)}, u32[]{:S(2)}, u32[]{:S(2)}) collective-permute-start(f32[32,1792]{1,0:T(8,128)S(1)} %get-tuple-element.29), channel_id=1, source_target_pairs={{0,2},{2,0},{1,3},{3,1},{4,6},{6,4},{5,7},{7,5},{8,10},{10,8},{9,1... | collective-permute-start | bytes 688136 | tf_op jit(solution)/shard_map/ppermute | solution.py:58
  13.3 0.0 collective-permute-done.1.piece
  13.3 0.9 %shard_map.40 = (f32[32,1792]{1,0:T(8,128)S(1)}, f32[32,1792]{1,0:T(8,128)S(1)}) custom-call(s32[6]{0:T(128)S(1)} %bitcast.9, f32[64,128]{1,0:T(8,128)S(1)} %collective-permute-done.1.piece, bf16[6,64,1792]{2,1,0:T(8,128)(2,1)S(1)} %get-tuple-element.20.high, bf16[6,64,1792]{2,1,0:T(8,128)(2,1)S(1)} %get-tuple-element.21.low), custom_call_target="tpu_custom_call" | custom-call | flops 1 | bytes 1 | tf_op jit(solution)/shard_map/pallas_call | solution.py:129
  14.2 0.6 %collective-permute-start.2 = (f32[32,1792]{1,0:T(8,128)S(1)}, f32[32,1792]{1,0:T(8,128)S(1)}, u32[]{:S(2)}, u32[]{:S(2)}) collective-permute-start(f32[32,1792]{1,0:T(8,128)S(1)} %get-tuple-element.26), channel_id=1, source_target_pairs={{0,2},{2,0},{1,3},{3,1},{4,6},{6,4},{5,7},{7,5},{8,10},{10,8},{9,1... | collective-permute-start | bytes 688136 | tf_op jit(solution)/shard_map/ppermute | solution.py:58
  14.8 0.9 %shard_map.39 = (f32[32,1792]{1,0:T(8,128)S(1)}, f32[32,1792]{1,0:T(8,128)S(1)}) custom-call(s32[6]{0:T(128)S(1)} %bitcast.10, f32[64,128]{1,0:T(8,128)S(1)} %get-tuple-element.19.piece, bf16[6,64,1792]{2,1,0:T(8,128)(2,1)S(1)} %get-tuple-element.20.high, bf16[6,64,1792]{2,1,0:T(8,128)(2,1)S(1)} %get-tuple-element.21.low), custom_call_target="tpu_custom_call" | custom-call | flops 1 | bytes 1 | tf_op jit(solution)/shard_map/pallas_call | solution.py:129
  15.7 1.6 %collective-permute-start = (f32[32,1792]{1,0:T(8,128)S(1)}, f32[32,1792]{1,0:T(8,128)S(1)}, u32[]{:S(2)}, u32[]{:S(2)}) collective-permute-start(f32[32,1792]{1,0:T(8,128)S(1)} %get-tuple-element.23), channel_id=1, source_target_pairs={{0,2},{2,0},{1,3},{3,1},{4,6},{6,4},{5,7},{7,5},{8,10},{10,8},{9,1... | collective-permute-start | bytes 688136 | tf_op jit(solution)/shard_map/ppermute | solution.py:58
  17.3 0.0 collective-permute-done.8
  17.3 2.6 %collective-permute-start.9 = (f32[32,1792]{1,0:T(8,128)S(1)}, f32[32,1792]{1,0:T(8,128)S(1)}, u32[]{:S(2)}, u32[]{:S(2)}) collective-permute-start(f32[32,1792]{1,0:T(8,128)S(1)} %add.26), channel_id=1, source_target_pairs={{0,8},{4,12},{8,0},{12,4},{1,9},{5,13},{9,1},{13,5},{2,10},{6,14},... | collective-permute-start | bytes 688136 | tf_op jit(solution)/shard_map/ppermute | solution.py:58
  19.9 1.9 %collective-permute-done.5 = f32[32,1792]{1,0:T(8,128)S(1)} collective-permute-done((f32[32,1792]{1,0:T(8,128)S(1)}, f32[32,1792]{1,0:T(8,128)S(1)}, u32[]{:S(2)}, u32[]{:S(2)}) %collective-permute-start.5) | collective-permute-done | bytes 229408 | tf_op jit(solution)/shard_map/ppermute | solution.py:58
  21.8 4.2 %collective-permute-start.6 = (f32[32,1792]{1,0:T(8,128)S(1)}, f32[32,1792]{1,0:T(8,128)S(1)}, u32[]{:S(2)}, u32[]{:S(2)}) collective-permute-start(f32[32,1792]{1,0:T(8,128)S(1)} %add.24), channel_id=1, source_target_pairs={{0,12},{4,8},{8,4},{12,0},{1,13},{5,9},{9,5},{13,1},{2,14},{6,10},... | collective-permute-start | bytes 688136 | tf_op jit(solution)/shard_map/ppermute | solution.py:58
  26.1 0.7 %collective-permute-done.2 = f32[32,1792]{1,0:T(8,128)S(1)} collective-permute-done((f32[32,1792]{1,0:T(8,128)S(1)}, f32[32,1792]{1,0:T(8,128)S(1)}, u32[]{:S(2)}, u32[]{:S(2)}) %collective-permute-start.2) | collective-permute-done | bytes 229408 | tf_op jit(solution)/shard_map/ppermute | solution.py:58
  26.8 1.8 %collective-permute-start.3 = (f32[32,1792]{1,0:T(8,128)S(1)}, f32[32,1792]{1,0:T(8,128)S(1)}, u32[]{:S(2)}, u32[]{:S(2)}) collective-permute-start(f32[32,1792]{1,0:T(8,128)S(1)} %add.22), channel_id=1, source_target_pairs={{0,4},{4,0},{8,12},{12,8},{1,5},{5,1},{9,13},{13,9},{2,6},{6,2},{1... | collective-permute-start | bytes 688136 | tf_op jit(solution)/shard_map/ppermute | solution.py:58
  28.6 1.3 %collective-permute-done = f32[32,1792]{1,0:T(8,128)S(1)} collective-permute-done((f32[32,1792]{1,0:T(8,128)S(1)}, f32[32,1792]{1,0:T(8,128)S(1)}, u32[]{:S(2)}, u32[]{:S(2)}) %collective-permute-start) | collective-permute-done | bytes 229408 | tf_op jit(solution)/shard_map/ppermute | solution.py:58
  29.9 4.4 %collective-permute-done.9 = f32[32,1792]{1,0:T(8,128)S(1)} collective-permute-done((f32[32,1792]{1,0:T(8,128)S(1)}, f32[32,1792]{1,0:T(8,128)S(1)}, u32[]{:S(2)}, u32[]{:S(2)}) %collective-permute-start.9) | collective-permute-done | bytes 229408 | tf_op jit(solution)/shard_map/ppermute | solution.py:58
  34.2 0.0 collective-permute-done.6
  34.2 2.7 %collective-permute-done.3 = f32[32,1792]{1,0:T(8,128)S(1)} collective-permute-done((f32[32,1792]{1,0:T(8,128)S(1)}, f32[32,1792]{1,0:T(8,128)S(1)}, u32[]{:S(2)}, u32[]{:S(2)}) %collective-permute-start.3) | collective-permute-done | bytes 229408 | tf_op jit(solution)/shard_map/ppermute | solution.py:58
  36.9 0.8 %add_bitcast_fusion = f32[1,32,1792]{2,1,0:T(8,128)} fusion(f32[32,1792]{1,0:T(8,128)S(1)} %collective-permute-done.9, f32[32,1792]{1,0:T(8,128)S(1)} %collective-permute-done.6, f32[32,1792]{1,0:T(8,128)S(1)} %collective-permute-done.3, f32[32,1792]{1,0:T(8,128)S(1)} %get-tuple-element.22, f32[32,1792]{1,0:T(8,128)S(1)} %collective-permute-done), kind=kLoop, calls=%fused_computation | loop fusion | flops 229376 | bytes 1376256 | tf_op jit(solution)/shard_map/reshape | solution.py:136
  (3 shorter events, 0.1 us)
Async XLA Ops:
  0.9 5.8 %copy-start = (f32[1,1,6,64,1792]{4,3,2,1,0:T(8,128)S(1)}, f32[1,1,6,64,1792]{4,3,2,1,0:T(8,128)}, u32[]{:S(2)}) copy-start(f32[1,1,6,64,1792]{4,3,2,1,0:T(8,128)} %param.3) | copy-start | bytes 8257540
  1.0 6.3 %collective-permute-start.7 = (f32[64,128]{1,0:T(8,128)S(1)}, f32[64,128]{1,0:T(8,128)S(1)}, u32[]{:S(2)}, u32[]{:S(2)}) collective-permute-start(f32[64,128]{1,0:T(8,128)S(1)} %get-tuple-element.30), channel_id=1, source_target_pairs={{0,8},{4,12},{8,0},{12,4},{1,9},{5,13},{9,1},{13,5},{2,10},{6,14},... | collective-permute-start | bytes 98312 | tf_op jit(solution)/shard_map/ppermute | solution.py:58
  5.1 5.7 %collective-permute-start.4 = (f32[64,128]{1,0:T(8,128)S(1)}, f32[64,128]{1,0:T(8,128)S(1)}, u32[]{:S(2)}, u32[]{:S(2)}) collective-permute-start(f32[64,128]{1,0:T(8,128)S(1)} %get-tuple-element.27), channel_id=1, source_target_pairs={{0,12},{4,8},{8,4},{12,0},{1,13},{5,9},{9,5},{13,1},{2,14},{6,10},... | collective-permute-start | bytes 98312 | tf_op jit(solution)/shard_map/ppermute | solution.py:58
  6.5 6.8 %collective-permute-start.1 = (f32[64,128]{1,0:T(8,128)S(1)}, f32[64,128]{1,0:T(8,128)S(1)}, u32[]{:S(2)}, u32[]{:S(2)}) collective-permute-start(f32[64,128]{1,0:T(8,128)S(1)} %get-tuple-element.24), channel_id=1, source_target_pairs={{0,4},{4,0},{8,12},{12,8},{1,5},{5,1},{9,13},{13,9},{2,6},{6,2},{1... | collective-permute-start | bytes 98312 | tf_op jit(solution)/shard_map/ppermute | solution.py:58
  6.7 0.7 %copy-start.1 = (s32[1,1,6]{2,1,0:T(1,128)S(1)}, s32[1,1,6]{2,1,0:T(1,128)}, u32[]{:S(2)}) copy-start(s32[1,1,6]{2,1,0:T(1,128)} %param.5) | copy-start | bytes 76
  8.3 9.0 %collective-permute-start.8 = (f32[32,1792]{1,0:T(8,128)S(1)}, f32[32,1792]{1,0:T(8,128)S(1)}, u32[]{:S(2)}, u32[]{:S(2)}) collective-permute-start(f32[32,1792]{1,0:T(8,128)S(1)} %get-tuple-element.32), channel_id=1, source_target_pairs={{0,2},{2,0},{1,3},{3,1},{4,6},{6,4},{5,7},{7,5},{8,10},{10,8},{9,1... | collective-permute-start | bytes 688136 | tf_op jit(solution)/shard_map/ppermute | solution.py:58
  11.7 10.1 %collective-permute-start.5 = (f32[32,1792]{1,0:T(8,128)S(1)}, f32[32,1792]{1,0:T(8,128)S(1)}, u32[]{:S(2)}, u32[]{:S(2)}) collective-permute-start(f32[32,1792]{1,0:T(8,128)S(1)} %get-tuple-element.29), channel_id=1, source_target_pairs={{0,2},{2,0},{1,3},{3,1},{4,6},{6,4},{5,7},{7,5},{8,10},{10,8},{9,1... | collective-permute-start | bytes 688136 | tf_op jit(solution)/shard_map/ppermute | solution.py:58
  14.2 12.5 %collective-permute-start.2 = (f32[32,1792]{1,0:T(8,128)S(1)}, f32[32,1792]{1,0:T(8,128)S(1)}, u32[]{:S(2)}, u32[]{:S(2)}) collective-permute-start(f32[32,1792]{1,0:T(8,128)S(1)} %get-tuple-element.26), channel_id=1, source_target_pairs={{0,2},{2,0},{1,3},{3,1},{4,6},{6,4},{5,7},{7,5},{8,10},{10,8},{9,1... | collective-permute-start | bytes 688136 | tf_op jit(solution)/shard_map/ppermute | solution.py:58
  15.7 14.1 %collective-permute-start = (f32[32,1792]{1,0:T(8,128)S(1)}, f32[32,1792]{1,0:T(8,128)S(1)}, u32[]{:S(2)}, u32[]{:S(2)}) collective-permute-start(f32[32,1792]{1,0:T(8,128)S(1)} %get-tuple-element.23), channel_id=1, source_target_pairs={{0,2},{2,0},{1,3},{3,1},{4,6},{6,4},{5,7},{7,5},{8,10},{10,8},{9,1... | collective-permute-start | bytes 688136 | tf_op jit(solution)/shard_map/ppermute | solution.py:58
  17.3 16.9 %collective-permute-start.9 = (f32[32,1792]{1,0:T(8,128)S(1)}, f32[32,1792]{1,0:T(8,128)S(1)}, u32[]{:S(2)}, u32[]{:S(2)}) collective-permute-start(f32[32,1792]{1,0:T(8,128)S(1)} %add.26), channel_id=1, source_target_pairs={{0,8},{4,12},{8,0},{12,4},{1,9},{5,13},{9,1},{13,5},{2,10},{6,14},... | collective-permute-start | bytes 688136 | tf_op jit(solution)/shard_map/ppermute | solution.py:58
  21.8 12.4 %collective-permute-start.6 = (f32[32,1792]{1,0:T(8,128)S(1)}, f32[32,1792]{1,0:T(8,128)S(1)}, u32[]{:S(2)}, u32[]{:S(2)}) collective-permute-start(f32[32,1792]{1,0:T(8,128)S(1)} %add.24), channel_id=1, source_target_pairs={{0,12},{4,8},{8,4},{12,0},{1,13},{5,9},{9,5},{13,1},{2,14},{6,10},... | collective-permute-start | bytes 688136 | tf_op jit(solution)/shard_map/ppermute | solution.py:58
  26.8 10.2 %collective-permute-start.3 = (f32[32,1792]{1,0:T(8,128)S(1)}, f32[32,1792]{1,0:T(8,128)S(1)}, u32[]{:S(2)}, u32[]{:S(2)}) collective-permute-start(f32[32,1792]{1,0:T(8,128)S(1)} %add.22), channel_id=1, source_target_pairs={{0,4},{4,0},{8,12},{12,8},{1,5},{5,1},{9,13},{13,9},{2,6},{6,2},{1... | collective-permute-start | bytes 688136 | tf_op jit(solution)/shard_map/ppermute | solution.py:58

commit v3 on v2

--- a/solution.py
+++ b/solution.py
@@ -9,6 +9,9 @@
 
 TILE = 64
 CAP = 2
+EARLY = {2: 512, 1: 896}
+COST = {'f0': 10, 'f1': 5, 'f2': 1, 'k3': 5, 'k1': 5}
+AFTER = {'a2': (('fold', 2),), 'fold1': (('s', 3),), 'a1': (('s', 3),)}
 PAIR = TILE * CAP
 VMEM_LIMIT = 32 * 1024 * 1024
 ANY = pl.BlockSpec(memory_space=pl.ANY)
@@ -77,24 +80,55 @@
     low[...] = value_low
 
 
-def partial_kernel(distance, owner, piece, high, low, send, own):
+def ordered(piece):
+    rows = piece.shape[0] // 2
+    rep = lax.axis_index("rep")
+    return jnp.concatenate([piece[pl.ds(pl.multiple_of(q * rows, rows), rows), :] for q in (1 - rep, rep)], axis=0)
+
+
+def doubled(value):
+    high, low = split(value)
+    return jnp.concatenate(
+        [jnp.concatenate([high, high], axis=1), jnp.concatenate([low, jnp.zeros_like(low)], axis=1)], axis=0
+    )
+
+
+def multiply(distance, owner, piece, high, low, start):
+    found = find(owner, lax.axis_index("tiles") ^ distance)
+    lane = lax.broadcasted_iota(jnp.int32, piece.shape, 1)
+    kept = jnp.where(lane < TILE, found[0][1], found[1][1]) == 1
+    left = doubled(jnp.where(kept, ordered(piece), 0.0))
+    right = jnp.concatenate([half[k, :, start:] for half in (high, low) for k, _ in found], axis=0)
+    product = jnp.dot(left, right, preferred_element_type=jnp.float32)
+    return product[: piece.shape[0]] + product[piece.shape[0] :]
+
+
+def partial_kernel(distance, owner, piece, high, low, *rest):
+    send, own = rest[0], rest[1]
     rows = own.shape[0]
-    target = lax.axis_index("tiles") ^ distance
-    rep = lax.axis_index("rep")
-    (first, has_first), (second, has_second) = find(owner, target)
-    lane = lax.broadcasted_iota(jnp.int32, (rows, PAIR), 1)
-    kept = jnp.where(lane < TILE, has_first, has_second) == 1
-    right_high = jnp.concatenate([high[first], high[second]], axis=0)
-    right_low = jnp.concatenate([low[first], low[second]], axis=0)
-    parts = []
-    for pair_of in (1 - rep, rep):
-        block = piece[pl.ds(pl.multiple_of(pair_of * rows, rows), rows), :]
-        parts.append(jnp.where(kept, block, 0.0))
-    left_high, left_low = split(jnp.concatenate(parts, axis=0))
-    dot = functools.partial(jnp.dot, preferred_element_type=jnp.float32)
-    product = dot(left_high, right_high) + (dot(left_high, right_low) + dot(left_low, right_high))
-    send[...] = product[:rows]
-    own[...] = product[rows:]
+    product = multiply(distance, owner, piece, high, low, 0)
+    cut = product.shape[1] - own.shape[1]
+    send[...] = product[:rows, cut:]
+    own[...] = product[rows:, cut:]
+    if cut:
+        rest[2][...] = product[:, :cut]
+
+
+def fold_kernel(send, own, early, *rest):
+    send_out, own_out = rest[-2:]
+    rows, width = own.shape[0], early.shape[1]
+    send_out[...] = send[...]
+    own_out[...] = own[...]
+    send_out[:, :width] += early[:rows]
+    own_out[:, :width] += early[rows:]
+
+
+def add_kernel(first, *rest):
+    *others, out = rest
+    out[...] = first[...]
+    for other in others:
+        skip = out.shape[1] - other.shape[1]
+        out[:, skip:] += other[...]
 
 
 def square_shards(amplitudes, integrals, tile_owner):
@@ -124,15 +158,49 @@
         cost_estimate=pl.CostEstimate(flops=1, bytes_accessed=1, transcendentals=0),
     )(stored)
 
-    sums = {}
-    for e in (1, 3, 2, 0):
-        send, own = call(functools.partial(partial_kernel, e), [f32(rows, columns)] * 2, [SMEM] + [VMEM] * 3)(
-            owner, pieces[e], high, low
+    def kernel(name, body, outs, ins, args, after=()):
+        waits = [everything[key] for key in after]
+
+        def run(*refs):
+            body(*refs[: len(args)], *refs[len(args) + len(waits) :])
+
+        return call(run, outs, ins + [ANY] * len(waits), (), int(COST.get(name, 0) * 1.15e9) + 1)(*args, *waits)
+
+    everything = {("j", e): pieces[e] for e in range(groups)}
+    def partial(e):
+        cut = EARLY.get(e, 0)
+        shapes = [f32(rows, columns - cut)] * 2 + ([f32(2 * rows, cut)] if cut else [])
+        waits = AFTER.get(e, ())
+        send, own, *more = kernel(
+            f"k{e}", functools.partial(partial_kernel, e), shapes, [SMEM] + [VMEM] * 3,
+            [owner, pieces[e], high, low], waits,
         )
-        sums[e] = own + exchange(send, "rep", 1)
-    out = sums[0]
-    for e in (1, 3, 2):
-        out = out + exchange(sums[e], "tiles", e)
+        everything["k", e] = own
+        if more:
+            early[e] = exchange(more[0], "tiles", e)
+        return (send, own) if e == 0 else (exchange(send, "rep", 1), own)
+
+    def finish(e, arrived, own):
+        (total,) = kernel(f"a{e}", add_kernel, [f32(*own.shape)], [VMEM] * 2, [own, arrived], AFTER.get(f"a{e}", ()))
+        everything["s", e] = total
+        return exchange(total, "tiles", e)
+
+    early = {}
+    parts = {e: partial(e) for e in (1, 3, 2, 0)}
+    send, own = parts[0]
+    got = {}
+    for step in (2, -2, -3, 1, -1):
+        if step in early:
+            send, own = kernel(
+                f"fold{step}", fold_kernel, [f32(rows, columns)] * 2, [VMEM] * 3, [send, own, early[step]], AFTER.get(f"fold{step}", ())
+            )
+            everything["fold", step] = own
+        else:
+            got[-step] = finish(-step, *parts[-step])
+    got[0] = exchange(send, "rep", 1)
+    out = own
+    for n, group in enumerate(((2,), (3,), (1, 0))):
+        (out,) = kernel(f"f{n}", add_kernel, [f32(rows, columns)], [VMEM] * (1 + len(group)), [out] + [got[e] for e in group])
     return out.reshape(1, rows, columns)
 
 

time: 37.8 us -> 34.6 us (0.915)
  waiting for transfers between devices: 11.8 us -> 9.39 us
  starting transfers between devices: 19.8 us -> 18.7 us
  other arithmetic: 0.86 us -> 0 us
  Pallas kernels: 4.25 us -> 4.98 us
    ppermute x10 -> x12, waiting for transfers between devices: 11.8 us -> 9.39 us  [exchange(): return lax.ppermute(value, axis, [(i, i ^ distance) for i in range(size)])]
    ppermute x10 -> x12, starting transfers between devices: 19.8 us -> 18.7 us  [exchange(): return lax.ppermute(value, axis, [(i, i ^ distance) for i in range(size)])]
    reshape x1 -> x0, other arithmetic: 0.76 us -> none  [square_shards(): return out.reshape(1, rows, columns)]
    pallas_call x4 -> x12, Pallas kernels: 3.61 us -> 4.34 us  [kernel(): call(run, outs, ins + [ANY] * len(waits), (), int(COST.get(name, 0) * 115...]
  transfers between devices with their start and end apart: 10 -> 12, of which waited for: 7 -> 6; matrix products, arithmetic and copies ran while one was open for 0% -> 0% of each run, Pallas kernels for 11% -> 12%
where the time goes in v3:
time: 34.6 us; the launch traced here: 34.1 us
  starting transfers between devices  18.7 us (54%)
  waiting for transfers between devices  9.39 us (27%)
  Pallas kernels  4.98 us (14%)
  local copies, waits for them, and re-layouts  0.92 us (3%)
    ppermute x12, starting transfers between devices, exchange(): return lax.ppermute(value, axis, [(i, i ^ distance) for i in range(size)])  18.7 us
    ppermute x12, waiting for transfers between devices, exchange(): return lax.ppermute(value, axis, [(i, i ^ distance) for i in range(size)])  9.39 us
    pallas_call x12, Pallas kernels, kernel(): call(run, outs, ins + [ANY] * len(waits), (), int(COST.get(name, 0) * 115...  4.34 us
    unnamed x5, local copies, waits for them, and re-layouts  0.92 us
  transfers between devices with their start and end apart: 12, of which 6 were waited for; matrix products, arithmetic and copies ran while one was open for 0% of the time, Pallas kernels for 12%

profile of v3, /device:TPU:0, one launch (start us, length us, event | category | flops | bytes accessed | tf_op | source)
XLA Modules:
  0.0 34.1 jit_solution(11451753613253382008)
XLA Ops:
  0.0 0.9 %copy.4 = f32[2,32,1,512]{3,1,2,0:T(8,128)S(1)} copy(f32[2,32,1,512]{3,2,1,0:T(1,128)} %param.4) | data formatting | bytes 262144
  0.9 0.0 copy-start
  0.9 0.1 shard_map.37
  1.0 4.1 %collective-permute-start = (f32[64,128]{1,0:T(8,128)S(1)}, f32[64,128]{1,0:T(8,128)S(1)}, u32[]{:S(2)}, u32[]{:S(2)}) collective-permute-start(f32[64,128]{1,0:T(8,128)S(1)} %get-tuple-element.30), channel_id=1, source_target_pairs={{0,8},{4,12},{8,0},{12,4},{1,9},{5,13},{9,1},{13,5},{2,10},{6,14},... | collective-permute-start | bytes 98312 | tf_op jit(solution)/shard_map/ppermute | solution.py:61
  5.1 1.3 %collective-permute-start.4 = (f32[64,128]{1,0:T(8,128)S(1)}, f32[64,128]{1,0:T(8,128)S(1)}, u32[]{:S(2)}, u32[]{:S(2)}) collective-permute-start(f32[64,128]{1,0:T(8,128)S(1)} %get-tuple-element.36), channel_id=1, source_target_pairs={{0,12},{4,8},{8,4},{12,0},{1,13},{5,9},{9,5},{13,1},{2,14},{6,10},... | collective-permute-start | bytes 98312 | tf_op jit(solution)/shard_map/ppermute | solution.py:61
  6.5 0.2 collective-permute-start.2
  6.7 0.0 copy-done
  6.7 0.0 copy-start.1
  6.7 0.6 %shard_map.38 = (bf16[6,64,1792]{2,1,0:T(8,128)(2,1)S(1)}, bf16[6,64,1792]{2,1,0:T(8,128)(2,1)S(1)}) custom-call(f32[6,64,1792]{2,1,0:T(8,128)S(1)} %bitcast.4), custom_call_target="tpu_custom_call" | custom-call | flops 1 | bytes 1 | tf_op jit(solution)/shard_map/pallas_call | solution.py:151
  7.3 0.1 collective-permute-done.refs_1_
  7.4 0.0 copy-done.1
  7.4 0.9 %shard_map.40 = (f32[32,1280]{1,0:T(8,128)S(1)}, f32[32,1280]{1,0:T(8,128)S(1)}, f32[64,512]{1,0:T(8,128)S(1)}) custom-call(s32[6]{0:T(128)S(1)} %bitcast.6, f32[64,128]{1,0:T(8,128)S(1)} %collective-permute-done.refs_1_, bf16[6,64,1792]{2,1,0:T(8,128)(2,1)S(1)} %get-tuple-element.26.refs_2_, bf16[6,64,1792]{2,1,0:T(8,128)(2,1)S(1)} %get-tuple-element.27.refs_3_), custom_call_target="tpu_custom_call" | custom-call | flops 1 | bytes 1 | tf_op jit(solution)/shard_map/pallas_call | solution.py:167
  8.2 3.0 %collective-permute-start.1 = (f32[64,512]{1,0:T(8,128)S(1)}, f32[64,512]{1,0:T(8,128)S(1)}, u32[]{:S(2)}, u32[]{:S(2)}) collective-permute-start(f32[64,512]{1,0:T(8,128)S(1)} %get-tuple-element.31), channel_id=1, source_target_pairs={{0,8},{4,12},{8,0},{12,4},{1,9},{5,13},{9,1},{13,5},{2,10},{6,14},... | collective-permute-start | bytes 393224 | tf_op jit(solution)/shard_map/ppermute | solution.py:61
  11.2 1.5 %collective-permute-start.6 = (f32[32,1280]{1,0:T(8,128)S(1)}, f32[32,1280]{1,0:T(8,128)S(1)}, u32[]{:S(2)}, u32[]{:S(2)}) collective-permute-start(f32[32,1280]{1,0:T(8,128)S(1)} %get-tuple-element.41), channel_id=1, source_target_pairs={{0,2},{2,0},{1,3},{3,1},{4,6},{6,4},{5,7},{7,5},{8,10},{10,8},{9,1... | collective-permute-start | bytes 491528 | tf_op jit(solution)/shard_map/ppermute | solution.py:61
  12.7 0.0 collective-permute-done.4.refs_1_
  12.7 0.9 %shard_map.43 = (f32[32,1792]{1,0:T(8,128)S(1)}, f32[32,1792]{1,0:T(8,128)S(1)}) custom-call(s32[6]{0:T(128)S(1)} %bitcast.7, f32[64,128]{1,0:T(8,128)S(1)} %collective-permute-done.4.refs_1_, bf16[6,64,1792]{2,1,0:T(8,128)(2,1)S(1)} %get-tuple-element.26.refs_2_, bf16[6,64,1792]{2,1,0:T(8,128)(2,1)S(1)} %get-tuple-element.27.refs_3_), custom_call_target="tpu_custom_call" | custom-call | flops 5750000128 | bytes 1 | tf_op jit(solution)/shard_map/pallas_call | solution.py:167
  13.6 0.6 %collective-permute-start.5 = (f32[32,1792]{1,0:T(8,128)S(1)}, f32[32,1792]{1,0:T(8,128)S(1)}, u32[]{:S(2)}, u32[]{:S(2)}) collective-permute-start(f32[32,1792]{1,0:T(8,128)S(1)} %get-tuple-element.38), channel_id=1, source_target_pairs={{0,2},{2,0},{1,3},{3,1},{4,6},{6,4},{5,7},{7,5},{8,10},{10,8},{9,1... | collective-permute-start | bytes 688136 | tf_op jit(solution)/shard_map/ppermute | solution.py:61
  14.2 0.0 collective-permute-done.2.refs_1_
  14.2 0.9 %shard_map.42 = (f32[32,896]{1,0:T(8,128)S(1)}, f32[32,896]{1,0:T(8,128)S(1)}, f32[64,896]{1,0:T(8,128)S(1)}) custom-call(s32[6]{0:T(128)S(1)} %bitcast.8, f32[64,128]{1,0:T(8,128)S(1)} %collective-permute-done.2.refs_1_, bf16[6,64,1792]{2,1,0:T(8,128)(2,1)S(1)} %get-tuple-element.26.refs_2_, bf16[6,64,1792]{2,1,0:T(8,128)(2,1)S(1)} %get-tuple-element.27.refs_3_), custom_call_target="tpu_custom_call" | custom-call | flops 5750000128 | bytes 1 | tf_op jit(solution)/shard_map/pallas_call | solution.py:167
  15.1 1.8 %collective-permute-start.3 = (f32[64,896]{1,0:T(8,128)S(1)}, f32[64,896]{1,0:T(8,128)S(1)}, u32[]{:S(2)}, u32[]{:S(2)}) collective-permute-start(f32[64,896]{1,0:T(8,128)S(1)} %get-tuple-element.35), channel_id=1, source_target_pairs={{0,4},{4,0},{8,12},{12,8},{1,5},{5,1},{9,13},{13,9},{2,6},{6,2},{1... | collective-permute-start | bytes 688136 | tf_op jit(solution)/shard_map/ppermute | solution.py:61
  16.9 0.9 %shard_map.39 = (f32[32,1792]{1,0:T(8,128)S(1)}, f32[32,1792]{1,0:T(8,128)S(1)}) custom-call(s32[6]{0:T(128)S(1)} %bitcast.9, f32[64,128]{1,0:T(8,128)S(1)} %get-tuple-element.25.refs_1_, bf16[6,64,1792]{2,1,0:T(8,128)(2,1)S(1)} %get-tuple-element.26.refs_2_, bf16[6,64,1792]{2,1,0:T(8,128)(2,1)S(1)} %get-tuple-element.27.refs_3_), custom_call_target="tpu_custom_call" | custom-call | flops 1 | bytes 1 | tf_op jit(solution)/shard_map/pallas_call | solution.py:167
  17.8 0.0 collective-permute-done.1.refs_2_
  17.8 0.5 %collective-permute-done.6.refs_1_ = f32[32,1280]{1,0:T(8,128)S(1)} collective-permute-done((f32[32,1280]{1,0:T(8,128)S(1)}, f32[32,1280]{1,0:T(8,128)S(1)}, u32[]{:S(2)}, u32[]{:S(2)}) %collective-permute-start.6) | collective-permute-done | bytes 163872 | tf_op jit(solution)/shard_map/ppermute | solution.py:61
  18.3 0.1 collective-permute-start.7
  18.4 1.7 %collective-permute-start.9 = (f32[32,896]{1,0:T(8,128)S(1)}, f32[32,896]{1,0:T(8,128)S(1)}, u32[]{:S(2)}, u32[]{:S(2)}) collective-permute-start(f32[32,896]{1,0:T(8,128)S(1)} %get-tuple-element.43), channel_id=1, source_target_pairs={{0,2},{2,0},{1,3},{3,1},{4,6},{6,4},{5,7},{7,5},{8,10},{10,8},{9,1... | collective-permute-start | bytes 344072 | tf_op jit(solution)/shard_map/ppermute | solution.py:61
  20.2 2.3 %collective-permute-done.5.refs_1_ = f32[32,1792]{1,0:T(8,128)S(1)} collective-permute-done((f32[32,1792]{1,0:T(8,128)S(1)}, f32[32,1792]{1,0:T(8,128)S(1)}, u32[]{:S(2)}, u32[]{:S(2)}) %collective-permute-start.5) | collective-permute-done | bytes 229408 | tf_op jit(solution)/shard_map/ppermute | solution.py:61
  22.5 1.2 %collective-permute-start.8 = (f32[32,1792]{1,0:T(8,128)S(1)}, f32[32,1792]{1,0:T(8,128)S(1)}, u32[]{:S(2)}, u32[]{:S(2)}) collective-permute-start(f32[32,1792]{1,0:T(8,128)S(1)} %shard_map.44.refs_3_.refs_2_), channel_id=1, source_target_pairs={{0,12},{4,8},{8,4},{12,0},{1,13},{5,9},{9,5},{13,1},{2,14},{6,10},... | collective-permute-start | bytes 688136 | tf_op jit(solution)/shard_map/ppermute | solution.py:61
  23.7 0.1 collective-permute-done.3.refs_2_
  23.8 2.1 %collective-permute-start.11 = (f32[32,1792]{1,0:T(8,128)S(1)}, f32[32,1792]{1,0:T(8,128)S(1)}, u32[]{:S(2)}, u32[]{:S(2)}) collective-permute-start(f32[32,1792]{1,0:T(8,128)S(1)} %get-tuple-element.44), channel_id=1, source_target_pairs={{0,2},{2,0},{1,3},{3,1},{4,6},{6,4},{5,7},{7,5},{8,10},{10,8},{9,1... | collective-permute-start | bytes 688136 | tf_op jit(solution)/shard_map/ppermute | solution.py:61
  25.9 0.0 collective-permute-done.9.refs_1_
  26.0 0.9 %collective-permute-start.10 = (f32[32,896]{1,0:T(8,128)S(1)}, f32[32,896]{1,0:T(8,128)S(1)}, u32[]{:S(2)}, u32[]{:S(2)}) collective-permute-start(f32[32,896]{1,0:T(8,128)S(1)} %shard_map.49), channel_id=1, source_target_pairs={{0,4},{4,0},{8,12},{12,8},{1,5},{5,1},{9,13},{13,9},{2,6},{6,2},{1... | collective-permute-start | bytes 344072 | tf_op jit(solution)/shard_map/ppermute | solution.py:61
  26.9 6.2 %collective-permute-done.7.refs_1_ = f32[32,1280]{1,0:T(8,128)S(1)} collective-permute-done((f32[32,1280]{1,0:T(8,128)S(1)}, f32[32,1280]{1,0:T(8,128)S(1)}, u32[]{:S(2)}, u32[]{:S(2)}) %collective-permute-start.7) | collective-permute-done | bytes 163872 | tf_op jit(solution)/shard_map/ppermute | solution.py:61
  33.1 0.0 collective-permute-done.8.refs_1_
  33.2 0.2 collective-permute-done.10.refs_1_
  33.4 0.0 collective-permute-done.11.refs_2_
  33.4 0.7 %shard_map.50 = f32[32,1792]{1,0:T(8,128)} custom-call(f32[32,1792]{1,0:T(8,128)S(1)} %shard_map.48.refs_0_, f32[32,896]{1,0:T(8,128)S(1)} %collective-permute-done.10.refs_1_, f32[32,1792]{1,0:T(8,128)S(1)} %collective-permute-done.11.refs_2_), custom_call_target="tpu_custom_call" | custom-call | flops 1150000000 | bytes 1 | tf_op jit(solution)/shard_map/pallas_call | solution.py:167
  (7 shorter events, 0.2 us)
Async XLA Ops:
  0.9 5.8 %copy-start = (f32[1,1,6,64,1792]{4,3,2,1,0:T(8,128)S(1)}, f32[1,1,6,64,1792]{4,3,2,1,0:T(8,128)}, u32[]{:S(2)}) copy-start(f32[1,1,6,64,1792]{4,3,2,1,0:T(8,128)} %param.3) | copy-start | bytes 8257540
  1.0 6.3 %collective-permute-start = (f32[64,128]{1,0:T(8,128)S(1)}, f32[64,128]{1,0:T(8,128)S(1)}, u32[]{:S(2)}, u32[]{:S(2)}) collective-permute-start(f32[64,128]{1,0:T(8,128)S(1)} %get-tuple-element.30), channel_id=1, source_target_pairs={{0,8},{4,12},{8,0},{12,4},{1,9},{5,13},{9,1},{13,5},{2,10},{6,14},... | collective-permute-start | bytes 98312 | tf_op jit(solution)/shard_map/ppermute | solution.py:61
  5.1 7.6 %collective-permute-start.4 = (f32[64,128]{1,0:T(8,128)S(1)}, f32[64,128]{1,0:T(8,128)S(1)}, u32[]{:S(2)}, u32[]{:S(2)}) collective-permute-start(f32[64,128]{1,0:T(8,128)S(1)} %get-tuple-element.36), channel_id=1, source_target_pairs={{0,12},{4,8},{8,4},{12,0},{1,13},{5,9},{9,5},{13,1},{2,14},{6,10},... | collective-permute-start | bytes 98312 | tf_op jit(solution)/shard_map/ppermute | solution.py:61
  6.5 7.7 %collective-permute-start.2 = (f32[64,128]{1,0:T(8,128)S(1)}, f32[64,128]{1,0:T(8,128)S(1)}, u32[]{:S(2)}, u32[]{:S(2)}) collective-permute-start(f32[64,128]{1,0:T(8,128)S(1)} %get-tuple-element.34), channel_id=1, source_target_pairs={{0,4},{4,0},{8,12},{12,8},{1,5},{5,1},{9,13},{13,9},{2,6},{6,2},{1... | collective-permute-start | bytes 98312 | tf_op jit(solution)/shard_map/ppermute | solution.py:61
  6.7 0.7 %copy-start.1 = (s32[1,1,6]{2,1,0:T(1,128)S(1)}, s32[1,1,6]{2,1,0:T(1,128)}, u32[]{:S(2)}) copy-start(s32[1,1,6]{2,1,0:T(1,128)} %param.5) | copy-start | bytes 76
  8.2 9.5 %collective-permute-start.1 = (f32[64,512]{1,0:T(8,128)S(1)}, f32[64,512]{1,0:T(8,128)S(1)}, u32[]{:S(2)}, u32[]{:S(2)}) collective-permute-start(f32[64,512]{1,0:T(8,128)S(1)} %get-tuple-element.31), channel_id=1, source_target_pairs={{0,8},{4,12},{8,0},{12,4},{1,9},{5,13},{9,1},{13,5},{2,10},{6,14},... | collective-permute-start | bytes 393224 | tf_op jit(solution)/shard_map/ppermute | solution.py:61
  11.2 7.1 %collective-permute-start.6 = (f32[32,1280]{1,0:T(8,128)S(1)}, f32[32,1280]{1,0:T(8,128)S(1)}, u32[]{:S(2)}, u32[]{:S(2)}) collective-permute-start(f32[32,1280]{1,0:T(8,128)S(1)} %get-tuple-element.41), channel_id=1, source_target_pairs={{0,2},{2,0},{1,3},{3,1},{4,6},{6,4},{5,7},{7,5},{8,10},{10,8},{9,1... | collective-permute-start | bytes 491528 | tf_op jit(solution)/shard_map/ppermute | solution.py:61
  13.6 8.9 %collective-permute-start.5 = (f32[32,1792]{1,0:T(8,128)S(1)}, f32[32,1792]{1,0:T(8,128)S(1)}, u32[]{:S(2)}, u32[]{:S(2)}) collective-permute-start(f32[32,1792]{1,0:T(8,128)S(1)} %get-tuple-element.38), channel_id=1, source_target_pairs={{0,2},{2,0},{1,3},{3,1},{4,6},{6,4},{5,7},{7,5},{8,10},{10,8},{9,1... | collective-permute-start | bytes 688136 | tf_op jit(solution)/shard_map/ppermute | solution.py:61
  15.1 8.7 %collective-permute-start.3 = (f32[64,896]{1,0:T(8,128)S(1)}, f32[64,896]{1,0:T(8,128)S(1)}, u32[]{:S(2)}, u32[]{:S(2)}) collective-permute-start(f32[64,896]{1,0:T(8,128)S(1)} %get-tuple-element.35), channel_id=1, source_target_pairs={{0,4},{4,0},{8,12},{12,8},{1,5},{5,1},{9,13},{13,9},{2,6},{6,2},{1... | collective-permute-start | bytes 688136 | tf_op jit(solution)/shard_map/ppermute | solution.py:61
  18.3 14.8 %collective-permute-start.7 = (f32[32,1280]{1,0:T(8,128)S(1)}, f32[32,1280]{1,0:T(8,128)S(1)}, u32[]{:S(2)}, u32[]{:S(2)}) collective-permute-start(f32[32,1280]{1,0:T(8,128)S(1)} %shard_map.46), channel_id=1, source_target_pairs={{0,8},{4,12},{8,0},{12,4},{1,9},{5,13},{9,1},{13,5},{2,10},{6,14},... | collective-permute-start | bytes 491528 | tf_op jit(solution)/shard_map/ppermute | solution.py:61
  18.4 7.5 %collective-permute-start.9 = (f32[32,896]{1,0:T(8,128)S(1)}, f32[32,896]{1,0:T(8,128)S(1)}, u32[]{:S(2)}, u32[]{:S(2)}) collective-permute-start(f32[32,896]{1,0:T(8,128)S(1)} %get-tuple-element.43), channel_id=1, source_target_pairs={{0,2},{2,0},{1,3},{3,1},{4,6},{6,4},{5,7},{7,5},{8,10},{10,8},{9,1... | collective-permute-start | bytes 344072 | tf_op jit(solution)/shard_map/ppermute | solution.py:61
  22.5 10.7 %collective-permute-start.8 = (f32[32,1792]{1,0:T(8,128)S(1)}, f32[32,1792]{1,0:T(8,128)S(1)}, u32[]{:S(2)}, u32[]{:S(2)}) collective-permute-start(f32[32,1792]{1,0:T(8,128)S(1)} %shard_map.44.refs_3_.refs_2_), channel_id=1, source_target_pairs={{0,12},{4,8},{8,4},{12,0},{1,13},{5,9},{9,5},{13,1},{2,14},{6,10},... | collective-permute-start | bytes 688136 | tf_op jit(solution)/shard_map/ppermute | solution.py:61
  23.8 9.6 %collective-permute-start.11 = (f32[32,1792]{1,0:T(8,128)S(1)}, f32[32,1792]{1,0:T(8,128)S(1)}, u32[]{:S(2)}, u32[]{:S(2)}) collective-permute-start(f32[32,1792]{1,0:T(8,128)S(1)} %get-tuple-element.44), channel_id=1, source_target_pairs={{0,2},{2,0},{1,3},{3,1},{4,6},{6,4},{5,7},{7,5},{8,10},{10,8},{9,1... | collective-permute-start | bytes 688136 | tf_op jit(solution)/shard_map/ppermute | solution.py:61
  26.0 7.4 %collective-permute-start.10 = (f32[32,896]{1,0:T(8,128)S(1)}, f32[32,896]{1,0:T(8,128)S(1)}, u32[]{:S(2)}, u32[]{:S(2)}) collective-permute-start(f32[32,896]{1,0:T(8,128)S(1)} %shard_map.49), channel_id=1, source_target_pairs={{0,4},{4,0},{8,12},{12,8},{1,5},{5,1},{9,13},{13,9},{2,6},{6,2},{1... | collective-permute-start | bytes 344072 | tf_op jit(solution)/shard_map/ppermute | solution.py:61

commit v4 on v3

--- a/solution.py
+++ b/solution.py
@@ -10,8 +10,9 @@
 TILE = 64
 CAP = 2
 EARLY = {2: 512, 1: 896}
-COST = {'f0': 10, 'f1': 5, 'f2': 1, 'k3': 5, 'k1': 5}
+COST = {'f0': 10, 'f1': 5, 'f2': 1, 'k3': 5, 'k1': 0}
 AFTER = {'a2': (('fold', 2),), 'fold1': (('s', 3),), 'a1': (('s', 3),)}
+APART = (2,)
 PAIR = TILE * CAP
 VMEM_LIMIT = 32 * 1024 * 1024
 ANY = pl.BlockSpec(memory_space=pl.ANY)
@@ -93,20 +94,21 @@
     )
 
 
-def multiply(distance, owner, piece, high, low, start):
-    found = find(owner, lax.axis_index("tiles") ^ distance)
-    lane = lax.broadcasted_iota(jnp.int32, piece.shape, 1)
-    kept = jnp.where(lane < TILE, found[0][1], found[1][1]) == 1
-    left = doubled(jnp.where(kept, ordered(piece), 0.0))
-    right = jnp.concatenate([half[k, :, start:] for half in (high, low) for k, _ in found], axis=0)
-    product = jnp.dot(left, right, preferred_element_type=jnp.float32)
-    return product[: piece.shape[0]] + product[piece.shape[0] :]
-
-
-def partial_kernel(distance, owner, piece, high, low, *rest):
+def sort_kernel(owner, stored, tiles):
+    here = lax.axis_index("tiles")
+    for distance in range(tiles.shape[0]):
+        for slot, (index, filled) in enumerate(find(owner, here ^ distance)):
+            tile = stored[index]
+            high, low = split(jnp.where(filled == 1, tile, jnp.zeros_like(tile)))
+            tiles[distance, slot * TILE : (slot + 1) * TILE, :] = high
+            tiles[distance, PAIR + slot * TILE : PAIR + (slot + 1) * TILE, :] = low
+
+
+def partial_kernel(distance, piece, tiles, *rest):
     send, own = rest[0], rest[1]
     rows = own.shape[0]
-    product = multiply(distance, owner, piece, high, low, 0)
+    product = jnp.dot(doubled(ordered(piece)), tiles[distance], preferred_element_type=jnp.float32)
+    product = product[: 2 * rows] + product[2 * rows :]
     cut = product.shape[1] - own.shape[1]
     send[...] = product[:rows, cut:]
     own[...] = product[rows:, cut:]
@@ -147,16 +149,11 @@
         10**10,
     )(matrix)
     pieces = [picked[0]] + [exchange(picked[e], "tiles", e) for e in range(1, groups)]
-    half = jax.ShapeDtypeStruct(stored.shape, jnp.bfloat16)
-    high, low = pl.pallas_call(
-        split_kernel,
-        out_shape=[half, half],
-        grid=(stored.shape[0],),
-        in_specs=[pl.BlockSpec((1,) + stored.shape[1:], lambda k: (k, 0, 0))],
-        out_specs=[pl.BlockSpec((1,) + stored.shape[1:], lambda k: (k, 0, 0))] * 2,
-        compiler_params=pltpu.CompilerParams(vmem_limit_bytes=VMEM_LIMIT),
-        cost_estimate=pl.CostEstimate(flops=1, bytes_accessed=1, transcendentals=0),
-    )(stored)
+    (tiles,) = call(
+        sort_kernel,
+        [jax.ShapeDtypeStruct((groups, 2 * PAIR, columns), jnp.bfloat16)],
+        [SMEM, VMEM],
+    )(owner, stored)
 
     def kernel(name, body, outs, ins, args, after=()):
         waits = [everything[key] for key in after]
@@ -172,8 +169,8 @@
         shapes = [f32(rows, columns - cut)] * 2 + ([f32(2 * rows, cut)] if cut else [])
         waits = AFTER.get(e, ())
         send, own, *more = kernel(
-            f"k{e}", functools.partial(partial_kernel, e), shapes, [SMEM] + [VMEM] * 3,
-            [owner, pieces[e], high, low], waits,
+            f"k{e}", functools.partial(partial_kernel, e), shapes, [VMEM] * 2,
+            [pieces[e], tiles], waits,
         )
         everything["k", e] = own
         if more:

time: 34.6 us -> 33.7 us (0.974); the launches traced: 34.1 us -> 33.6 us
  Pallas kernels: 4.98 us -> 3.18 us
  waiting for transfers between devices: 9.39 us -> 11.1 us
  starting transfers between devices: 18.7 us -> 18.2 us
    pallas_call x12, Pallas kernels: 4.34 us -> 2.07 us  [kernel(): call(run, outs, ins + [ANY] * len(waits), (), int(COST.get(name, 0) * 115...]
    ppermute x12, waiting for transfers between devices: 9.39 us -> 11.1 us  [exchange(): return lax.ppermute(value, axis, [(i, i ^ distance) for i in range(size)])]
    pallas_call x1, Pallas kernels: 0.55 us -> 1.03 us  [square_shards(): call(sort_kernel, [jax.ShapeDtypeStruct((groups, 2 * PAIR, columns), jnp....]
    ppermute x12, starting transfers between devices: 18.7 us -> 18.2 us  [exchange(): return lax.ppermute(value, axis, [(i, i ^ distance) for i in range(size)])]
  transfers between devices with their start and end apart: 12 -> 12, of which waited for: 6 -> 4; matrix products, arithmetic and copies ran while one was open for 0% -> 0% of each run, Pallas kernels for 12% -> 7%
where the time goes in v4:
time: 33.7 us; the launch traced here: 33.6 us
  starting transfers between devices  18.2 us (54%)
  waiting for transfers between devices  11.1 us (33%)
  Pallas kernels  3.18 us (9%)
  local copies, waits for them, and re-layouts  0.93 us (3%)
    ppermute x12, starting transfers between devices, exchange(): return lax.ppermute(value, axis, [(i, i ^ distance) for i in range(size)])  18.2 us
    ppermute x12, waiting for transfers between devices, exchange(): return lax.ppermute(value, axis, [(i, i ^ distance) for i in range(size)])  11.1 us
    pallas_call x12, Pallas kernels, kernel(): call(run, outs, ins + [ANY] * len(waits), (), int(COST.get(name, 0) * 115...  2.07 us
    pallas_call x1, Pallas kernels, square_shards(): call(sort_kernel, [jax.ShapeDtypeStruct((groups, 2 * PAIR, columns), jnp....  1.03 us
    unnamed x5, local copies, waits for them, and re-layouts  0.93 us
  transfers between devices with their start and end apart: 12, of which 4 were waited for; matrix products, arithmetic and copies ran while one was open for 0% of the time, Pallas kernels for 7%

profile of v4, /device:TPU:0, one launch (start us, length us, event | category | flops | bytes accessed | tf_op | source)
XLA Modules:
  0.0 33.6 jit_solution(17165692658531230867)
XLA Ops:
  0.0 0.9 %copy.4 = f32[2,32,1,512]{3,1,2,0:T(8,128)S(1)} copy(f32[2,32,1,512]{3,2,1,0:T(1,128)} %param.4) | data formatting | bytes 262144
  0.9 0.0 copy-start
  0.9 0.0 copy-start.1
  0.9 0.1 shard_map.37
  1.0 4.1 %collective-permute-start = (f32[64,128]{1,0:T(8,128)S(1)}, f32[64,128]{1,0:T(8,128)S(1)}, u32[]{:S(2)}, u32[]{:S(2)}) collective-permute-start(f32[64,128]{1,0:T(8,128)S(1)} %get-tuple-element.26), channel_id=1, source_target_pairs={{0,8},{4,12},{8,0},{12,4},{1,9},{5,13},{9,1},{13,5},{2,10},{6,14},... | collective-permute-start | bytes 98312 | tf_op jit(solution)/shard_map/ppermute | solution.py:62
  5.1 1.3 %collective-permute-start.4 = (f32[64,128]{1,0:T(8,128)S(1)}, f32[64,128]{1,0:T(8,128)S(1)}, u32[]{:S(2)}, u32[]{:S(2)}) collective-permute-start(f32[64,128]{1,0:T(8,128)S(1)} %get-tuple-element.32), channel_id=1, source_target_pairs={{0,12},{4,8},{8,4},{12,0},{1,13},{5,9},{9,5},{13,1},{2,14},{6,10},... | collective-permute-start | bytes 98312 | tf_op jit(solution)/shard_map/ppermute | solution.py:62
  6.5 0.2 collective-permute-start.2
  6.7 0.0 copy-done
  6.7 0.0 copy-done.1
  6.7 1.0 %shard_map.38.refs_1_ = bf16[4,256,1792]{2,1,0:T(8,128)(2,1)S(1)} custom-call(s32[6]{0:T(128)S(1)} %bitcast.6, f32[6,64,1792]{2,1,0:T(8,128)S(1)} %bitcast.4), custom_call_target="tpu_custom_call" | custom-call | flops 1 | bytes 1 | tf_op jit(solution)/shard_map/pallas_call | solution.py:152
  7.8 0.0 collective-permute-done.refs_0_
  7.8 0.3 shard_map.40
  8.1 2.9 %collective-permute-start.1 = (f32[64,512]{1,0:T(8,128)S(1)}, f32[64,512]{1,0:T(8,128)S(1)}, u32[]{:S(2)}, u32[]{:S(2)}) collective-permute-start(f32[64,512]{1,0:T(8,128)S(1)} %get-tuple-element.27), channel_id=1, source_target_pairs={{0,8},{4,12},{8,0},{12,4},{1,9},{5,13},{9,1},{13,5},{2,10},{6,14},... | collective-permute-start | bytes 393224 | tf_op jit(solution)/shard_map/ppermute | solution.py:62
  10.9 1.5 %collective-permute-start.6 = (f32[32,1280]{1,0:T(8,128)S(1)}, f32[32,1280]{1,0:T(8,128)S(1)}, u32[]{:S(2)}, u32[]{:S(2)}) collective-permute-start(f32[32,1280]{1,0:T(8,128)S(1)} %get-tuple-element.37), channel_id=1, source_target_pairs={{0,2},{2,0},{1,3},{3,1},{4,6},{6,4},{5,7},{7,5},{8,10},{10,8},{9,1... | collective-permute-start | bytes 491528 | tf_op jit(solution)/shard_map/ppermute | solution.py:62
  12.4 0.0 collective-permute-done.4.refs_0_
  12.4 0.3 shard_map.43
  12.7 0.6 %collective-permute-start.5 = (f32[32,1792]{1,0:T(8,128)S(1)}, f32[32,1792]{1,0:T(8,128)S(1)}, u32[]{:S(2)}, u32[]{:S(2)}) collective-permute-start(f32[32,1792]{1,0:T(8,128)S(1)} %get-tuple-element.34), channel_id=1, source_target_pairs={{0,2},{2,0},{1,3},{3,1},{4,6},{6,4},{5,7},{7,5},{8,10},{10,8},{9,1... | collective-permute-start | bytes 688136 | tf_op jit(solution)/shard_map/ppermute | solution.py:62
  13.3 0.0 collective-permute-done.2.refs_0_
  13.3 0.3 shard_map.42
  13.6 1.6 %collective-permute-start.3 = (f32[64,896]{1,0:T(8,128)S(1)}, f32[64,896]{1,0:T(8,128)S(1)}, u32[]{:S(2)}, u32[]{:S(2)}) collective-permute-start(f32[64,896]{1,0:T(8,128)S(1)} %get-tuple-element.31), channel_id=1, source_target_pairs={{0,4},{4,0},{8,12},{12,8},{1,5},{5,1},{9,13},{13,9},{2,6},{6,2},{1... | collective-permute-start | bytes 688136 | tf_op jit(solution)/shard_map/ppermute | solution.py:62
  15.2 0.3 shard_map.39
  15.5 1.1 %collective-permute-done.1.refs_2_ = f32[64,512]{1,0:T(8,128)S(1)} collective-permute-done((f32[64,512]{1,0:T(8,128)S(1)}, f32[64,512]{1,0:T(8,128)S(1)}, u32[]{:S(2)}, u32[]{:S(2)}) %collective-permute-start.1) | collective-permute-done | bytes 131104 | tf_op jit(solution)/shard_map/ppermute | solution.py:62
  16.7 1.4 %collective-permute-done.6.refs_1_ = f32[32,1280]{1,0:T(8,128)S(1)} collective-permute-done((f32[32,1280]{1,0:T(8,128)S(1)}, f32[32,1280]{1,0:T(8,128)S(1)}, u32[]{:S(2)}, u32[]{:S(2)}) %collective-permute-start.6) | collective-permute-done | bytes 163872 | tf_op jit(solution)/shard_map/ppermute | solution.py:62
  18.1 0.2 collective-permute-start.7
  18.3 1.5 %collective-permute-start.9 = (f32[32,896]{1,0:T(8,128)S(1)}, f32[32,896]{1,0:T(8,128)S(1)}, u32[]{:S(2)}, u32[]{:S(2)}) collective-permute-start(f32[32,896]{1,0:T(8,128)S(1)} %get-tuple-element.39), channel_id=1, source_target_pairs={{0,2},{2,0},{1,3},{3,1},{4,6},{6,4},{5,7},{7,5},{8,10},{10,8},{9,1... | collective-permute-start | bytes 344072 | tf_op jit(solution)/shard_map/ppermute | solution.py:62
  19.8 2.1 %collective-permute-done.5.refs_1_ = f32[32,1792]{1,0:T(8,128)S(1)} collective-permute-done((f32[32,1792]{1,0:T(8,128)S(1)}, f32[32,1792]{1,0:T(8,128)S(1)}, u32[]{:S(2)}, u32[]{:S(2)}) %collective-permute-start.5) | collective-permute-done | bytes 229408 | tf_op jit(solution)/shard_map/ppermute | solution.py:62
  21.9 1.4 %collective-permute-start.8 = (f32[32,1792]{1,0:T(8,128)S(1)}, f32[32,1792]{1,0:T(8,128)S(1)}, u32[]{:S(2)}, u32[]{:S(2)}) collective-permute-start(f32[32,1792]{1,0:T(8,128)S(1)} %shard_map.44.refs_3_.refs_2_), channel_id=1, source_target_pairs={{0,12},{4,8},{8,4},{12,0},{1,13},{5,9},{9,5},{13,1},{2,14},{6,10},... | collective-permute-start | bytes 688136 | tf_op jit(solution)/shard_map/ppermute | solution.py:62
  23.3 0.0 collective-permute-done.3.refs_2_
  23.4 1.6 %collective-permute-start.11 = (f32[32,1792]{1,0:T(8,128)S(1)}, f32[32,1792]{1,0:T(8,128)S(1)}, u32[]{:S(2)}, u32[]{:S(2)}) collective-permute-start(f32[32,1792]{1,0:T(8,128)S(1)} %get-tuple-element.40), channel_id=1, source_target_pairs={{0,2},{2,0},{1,3},{3,1},{4,6},{6,4},{5,7},{7,5},{8,10},{10,8},{9,1... | collective-permute-start | bytes 688136 | tf_op jit(solution)/shard_map/ppermute | solution.py:62
  24.9 0.0 collective-permute-done.9.refs_1_
  25.0 1.4 %collective-permute-start.10 = (f32[32,896]{1,0:T(8,128)S(1)}, f32[32,896]{1,0:T(8,128)S(1)}, u32[]{:S(2)}, u32[]{:S(2)}) collective-permute-start(f32[32,896]{1,0:T(8,128)S(1)} %shard_map.49), channel_id=1, source_target_pairs={{0,4},{4,0},{8,12},{12,8},{1,5},{5,1},{9,13},{13,9},{2,6},{6,2},{1... | collective-permute-start | bytes 344072 | tf_op jit(solution)/shard_map/ppermute | solution.py:62
  26.3 6.4 %collective-permute-done.7.refs_1_ = f32[32,1280]{1,0:T(8,128)S(1)} collective-permute-done((f32[32,1280]{1,0:T(8,128)S(1)}, f32[32,1280]{1,0:T(8,128)S(1)}, u32[]{:S(2)}, u32[]{:S(2)}) %collective-permute-start.7) | collective-permute-done | bytes 163872 | tf_op jit(solution)/shard_map/ppermute | solution.py:62
  32.8 0.0 collective-permute-done.8.refs_1_
  32.9 0.0 collective-permute-done.10.refs_1_
  32.9 0.0 collective-permute-done.11.refs_2_
  32.9 0.7 %shard_map.50 = f32[32,1792]{1,0:T(8,128)} custom-call(f32[32,1792]{1,0:T(8,128)S(1)} %shard_map.48.refs_0_, f32[32,896]{1,0:T(8,128)S(1)} %collective-permute-done.10.refs_1_, f32[32,1792]{1,0:T(8,128)S(1)} %collective-permute-done.11.refs_2_), custom_call_target="tpu_custom_call" | custom-call | flops 1150000000 | bytes 1 | tf_op jit(solution)/shard_map/pallas_call | solution.py:164
  (7 shorter events, 0.2 us)
Async XLA Ops:
  0.9 5.8 %copy-start = (f32[1,1,6,64,1792]{4,3,2,1,0:T(8,128)S(1)}, f32[1,1,6,64,1792]{4,3,2,1,0:T(8,128)}, u32[]{:S(2)}) copy-start(f32[1,1,6,64,1792]{4,3,2,1,0:T(8,128)} %param.3) | copy-start | bytes 8257540
  0.9 5.8 %copy-start.1 = (s32[1,1,6]{2,1,0:T(1,128)S(1)}, s32[1,1,6]{2,1,0:T(1,128)}, u32[]{:S(2)}) copy-start(s32[1,1,6]{2,1,0:T(1,128)} %param.5) | copy-start | bytes 76
  1.0 6.7 %collective-permute-start = (f32[64,128]{1,0:T(8,128)S(1)}, f32[64,128]{1,0:T(8,128)S(1)}, u32[]{:S(2)}, u32[]{:S(2)}) collective-permute-start(f32[64,128]{1,0:T(8,128)S(1)} %get-tuple-element.26), channel_id=1, source_target_pairs={{0,8},{4,12},{8,0},{12,4},{1,9},{5,13},{9,1},{13,5},{2,10},{6,14},... | collective-permute-start | bytes 98312 | tf_op jit(solution)/shard_map/ppermute | solution.py:62
  5.1 7.3 %collective-permute-start.4 = (f32[64,128]{1,0:T(8,128)S(1)}, f32[64,128]{1,0:T(8,128)S(1)}, u32[]{:S(2)}, u32[]{:S(2)}) collective-permute-start(f32[64,128]{1,0:T(8,128)S(1)} %get-tuple-element.32), channel_id=1, source_target_pairs={{0,12},{4,8},{8,4},{12,0},{1,13},{5,9},{9,5},{13,1},{2,14},{6,10},... | collective-permute-start | bytes 98312 | tf_op jit(solution)/shard_map/ppermute | solution.py:62
  6.5 6.9 %collective-permute-start.2 = (f32[64,128]{1,0:T(8,128)S(1)}, f32[64,128]{1,0:T(8,128)S(1)}, u32[]{:S(2)}, u32[]{:S(2)}) collective-permute-start(f32[64,128]{1,0:T(8,128)S(1)} %get-tuple-element.30), channel_id=1, source_target_pairs={{0,4},{4,0},{8,12},{12,8},{1,5},{5,1},{9,13},{13,9},{2,6},{6,2},{1... | collective-permute-start | bytes 98312 | tf_op jit(solution)/shard_map/ppermute | solution.py:62
  8.1 8.6 %collective-permute-start.1 = (f32[64,512]{1,0:T(8,128)S(1)}, f32[64,512]{1,0:T(8,128)S(1)}, u32[]{:S(2)}, u32[]{:S(2)}) collective-permute-start(f32[64,512]{1,0:T(8,128)S(1)} %get-tuple-element.27), channel_id=1, source_target_pairs={{0,8},{4,12},{8,0},{12,4},{1,9},{5,13},{9,1},{13,5},{2,10},{6,14},... | collective-permute-start | bytes 393224 | tf_op jit(solution)/shard_map/ppermute | solution.py:62
  10.9 7.1 %collective-permute-start.6 = (f32[32,1280]{1,0:T(8,128)S(1)}, f32[32,1280]{1,0:T(8,128)S(1)}, u32[]{:S(2)}, u32[]{:S(2)}) collective-permute-start(f32[32,1280]{1,0:T(8,128)S(1)} %get-tuple-element.37), channel_id=1, source_target_pairs={{0,2},{2,0},{1,3},{3,1},{4,6},{6,4},{5,7},{7,5},{8,10},{10,8},{9,1... | collective-permute-start | bytes 491528 | tf_op jit(solution)/shard_map/ppermute | solution.py:62
  12.7 9.2 %collective-permute-start.5 = (f32[32,1792]{1,0:T(8,128)S(1)}, f32[32,1792]{1,0:T(8,128)S(1)}, u32[]{:S(2)}, u32[]{:S(2)}) collective-permute-start(f32[32,1792]{1,0:T(8,128)S(1)} %get-tuple-element.34), channel_id=1, source_target_pairs={{0,2},{2,0},{1,3},{3,1},{4,6},{6,4},{5,7},{7,5},{8,10},{10,8},{9,1... | collective-permute-start | bytes 688136 | tf_op jit(solution)/shard_map/ppermute | solution.py:62
  13.6 9.7 %collective-permute-start.3 = (f32[64,896]{1,0:T(8,128)S(1)}, f32[64,896]{1,0:T(8,128)S(1)}, u32[]{:S(2)}, u32[]{:S(2)}) collective-permute-start(f32[64,896]{1,0:T(8,128)S(1)} %get-tuple-element.31), channel_id=1, source_target_pairs={{0,4},{4,0},{8,12},{12,8},{1,5},{5,1},{9,13},{13,9},{2,6},{6,2},{1... | collective-permute-start | bytes 688136 | tf_op jit(solution)/shard_map/ppermute | solution.py:62
  18.1 14.7 %collective-permute-start.7 = (f32[32,1280]{1,0:T(8,128)S(1)}, f32[32,1280]{1,0:T(8,128)S(1)}, u32[]{:S(2)}, u32[]{:S(2)}) collective-permute-start(f32[32,1280]{1,0:T(8,128)S(1)} %shard_map.46), channel_id=1, source_target_pairs={{0,8},{4,12},{8,0},{12,4},{1,9},{5,13},{9,1},{13,5},{2,10},{6,14},... | collective-permute-start | bytes 491528 | tf_op jit(solution)/shard_map/ppermute | solution.py:62
  18.3 6.7 %collective-permute-start.9 = (f32[32,896]{1,0:T(8,128)S(1)}, f32[32,896]{1,0:T(8,128)S(1)}, u32[]{:S(2)}, u32[]{:S(2)}) collective-permute-start(f32[32,896]{1,0:T(8,128)S(1)} %get-tuple-element.39), channel_id=1, source_target_pairs={{0,2},{2,0},{1,3},{3,1},{4,6},{6,4},{5,7},{7,5},{8,10},{10,8},{9,1... | collective-permute-start | bytes 344072 | tf_op jit(solution)/shard_map/ppermute | solution.py:62
  21.9 10.9 %collective-permute-start.8 = (f32[32,1792]{1,0:T(8,128)S(1)}, f32[32,1792]{1,0:T(8,128)S(1)}, u32[]{:S(2)}, u32[]{:S(2)}) collective-permute-start(f32[32,1792]{1,0:T(8,128)S(1)} %shard_map.44.refs_3_.refs_2_), channel_id=1, source_target_pairs={{0,12},{4,8},{8,4},{12,0},{1,13},{5,9},{9,5},{13,1},{2,14},{6,10},... | collective-permute-start | bytes 688136 | tf_op jit(solution)/shard_map/ppermute | solution.py:62
  23.4 9.5 %collective-permute-start.11 = (f32[32,1792]{1,0:T(8,128)S(1)}, f32[32,1792]{1,0:T(8,128)S(1)}, u32[]{:S(2)}, u32[]{:S(2)}) collective-permute-start(f32[32,1792]{1,0:T(8,128)S(1)} %get-tuple-element.40), channel_id=1, source_target_pairs={{0,2},{2,0},{1,3},{3,1},{4,6},{6,4},{5,7},{7,5},{8,10},{10,8},{9,1... | collective-permute-start | bytes 688136 | tf_op jit(solution)/shard_map/ppermute | solution.py:62
  25.0 7.9 %collective-permute-start.10 = (f32[32,896]{1,0:T(8,128)S(1)}, f32[32,896]{1,0:T(8,128)S(1)}, u32[]{:S(2)}, u32[]{:S(2)}) collective-permute-start(f32[32,896]{1,0:T(8,128)S(1)} %shard_map.49), channel_id=1, source_target_pairs={{0,4},{4,0},{8,12},{12,8},{1,5},{5,1},{9,13},{13,9},{2,6},{6,2},{1... | collective-permute-start | bytes 344072 | tf_op jit(solution)/shard_map/ppermute | solution.py:62
